TPU v7x, 512 devices: a whole 4x8x8 slice. The times are simulated.
512 devices in a mesh: grp: 8 (over x, core), leaf: 64 (over z, y).
Axes of the slice: x: 4, y: 8, z: 8, core: 2. Of those that a mesh axis runs over, the one named last changes fastest.
Arguments:
- self_blocks: bfloat16 [1024, 512, 512], P(('grp', 'leaf')), as said below
- near_blocks: bfloat16 [1024, 1, 512, 512], P(('grp', 'leaf')), may hold values from -6 to 6
- leaf_basis: bfloat16 [1024, 512, 512], P(('grp', 'leaf')), may hold values from -0.25 to 0.25
- transfer: bfloat16 [1024, 16, 128, 128], P(('grp', 'leaf')), may hold values from -0.5 to 0.5
- near_list: int32 [1024, 1], P(('grp', 'leaf')), may hold values from 0 to 1023, as said below
- adm_list: int32 [1024, 16], P(('grp', 'leaf')), may hold values from 0 to 63, all different within a row; in each aligned block of 2 rows (0 to 1, 2 to 3, ...) at most 2 rows name the same one
- parent_kernel: bfloat16 [512, 128, 128], P(('grp', 'leaf')), may hold values from -0.00390625 to 0.00390625
- chain_coupling: float32 [8, 128, 128], P('grp'), may hold values from -0.5 to 0.5
Outputs:
- leaf_panels: float32 [1024, 128, 128], P(('grp', 'leaf'))
- parent_panels: float32 [512, 128, 128], P(('grp', 'leaf'))
- top_panels: float32 [8, 128, 128], P('grp')
Inputs may be any that keep to these rules, and one draw needn't show every extreme that they name: self_blocks are symmetric and strictly diagonally dominant with positive diagonal. `near_list`: each entry names a leaf held by a device next to the leaf's own device along leaf, in the same subtree. `adm_list`: each leaf names 16 different parents of its own subtree; parent p of a subtree is held by the device at place p along leaf; some parents are named far more often than others.
All inputs are finite; a program needn't handle non-finite values.
Results may differ from a plain program's by a relative error of at most 0.012.
Values may be sent and summed in bfloat16 or wider, within the bound.
A program may use at most 64 MiB of HBM per device.

v0:
```python
import jax
import jax.numpy as jnp
from jax import lax
from jax.sharding import PartitionSpec as P

highest = lax.Precision.HIGHEST


def with_halo(value, sides, width):
    for axis, dim in sides:
        devices, length = (lax.axis_size(axis), value.shape[dim])
        up = [(i, (i + 1) % devices) for i in range(devices - 1)]
        down = [(j, i) for i, j in up]
        last = lax.slice_in_dim(value, length - width, length, axis=dim)
        initial = lax.slice_in_dim(value, 0, width, axis=dim)
        before = lax.ppermute(last, axis, up)
        after = lax.ppermute(initial, axis, down)
        value = jnp.concatenate([before, value, after], axis=dim)
    return value


def from_behind(value, axis, by):
    devices = lax.axis_size(axis)
    pairs = [(i, i + by) for i in range(devices) if 0 <= i + by < devices]
    return lax.ppermute(value, axis, pairs)


def solve_block(factor, right_side):
    return jax.scipy.linalg.cho_solve((factor, True), right_side)


def eliminate(blocks, basis, redundant):
    projected = jnp.einsum(
        "lbq,lbc->lqc", basis, blocks, preferred_element_type=jnp.float32
    ).astype(jnp.bfloat16)
    reduced = jnp.einsum("lqc,lcp->lqp", projected, basis, preferred_element_type=jnp.float32)
    inner_block = reduced[:, :redundant, :redundant]
    upper_block = reduced[:, :redundant, redundant:]
    lower_block = reduced[:, redundant:, :redundant]
    corner = reduced[:, redundant:, redundant:]
    factor = jnp.linalg.cholesky(inner_block)
    solved = jax.vmap(solve_block)(factor, upper_block)
    return corner - jnp.einsum("lkr,lrm->lkm", lower_block, solved, precision=highest)


def advance(carried, mapping, addend):
    return (
        jnp.dot(mapping.T, jnp.dot(carried, mapping, precision=highest), precision=highest) + addend
    )


def per_device(
    self_blocks,
    near_blocks,
    leaf_basis,
    transfer,
    near_list,
    adm_list,
    parent_kernel,
    chain_coupling,
):
    leaf_count = self_blocks.shape[0]
    leaf_width = self_blocks.shape[1]
    skeleton_rank = transfer.shape[2]
    link_count = near_blocks.shape[1]
    redundant = leaf_width - skeleton_rank
    group_size = lax.axis_size("leaf")
    skeleton = leaf_basis[:, :, redundant:]
    beside_all = with_halo(skeleton, (("leaf", 0),), leaf_count)
    schur_block = eliminate(self_blocks, leaf_basis, redundant)
    first_leaf = (
        lax.axis_index("grp") * group_size + lax.axis_index("leaf")
    ) * leaf_count - leaf_count
    local_ids = (near_list - first_leaf).reshape(-1)
    partners = jnp.take(beside_all, local_ids, axis=0).reshape(
        leaf_count, link_count, leaf_width, skeleton_rank
    )
    facing = jnp.einsum(
        "lbk,ljbc->ljkc", skeleton, near_blocks, preferred_element_type=jnp.float32
    ).astype(jnp.bfloat16)
    coupling = jnp.einsum("ljkc,ljcm->lkm", facing, partners, preferred_element_type=jnp.float32)
    lowered = schur_block.astype(jnp.bfloat16)
    lifted = jnp.einsum(
        "lkm,lamn->lakn", lowered, transfer, preferred_element_type=jnp.float32
    ).astype(jnp.bfloat16)
    targets = (
        adm_list[:, :, None] == jnp.arange(group_size, dtype=jnp.int32)[None, None, :]
    ).astype(jnp.bfloat16)
    outgoing = jnp.einsum(
        "lan,lakm->nlkm", targets, lifted, preferred_element_type=jnp.float32
    ).astype(jnp.bfloat16)
    kernel = parent_kernel[0]
    pieces = lax.all_to_all(outgoing, "leaf", split_axis=0, concat_axis=0, tiled=True)
    mixture = jnp.einsum(
        "km,sime->sike", kernel, pieces, preferred_element_type=jnp.float32
    ).astype(jnp.bfloat16)
    received = jnp.einsum("simk,sime->ike", pieces, mixture, preferred_element_type=jnp.float32)
    parent = jnp.sum(received, axis=0, keepdims=True)
    group_root = lax.psum(parent, "leaf")[0] / group_size
    identity = jnp.eye(skeleton_rank, dtype=jnp.float32)
    step_map = 0.8 * identity + 0.5 * chain_coupling[0]
    top_panel = group_root
    for section in range(lax.axis_size("grp") - 1):
        earlier = from_behind(top_panel, "grp", 1)
        top_panel = advance(earlier, step_map, group_root)
    return (schur_block + coupling, parent, top_panel[None])


def solution(mesh):
    return jax.shard_map(
        per_device,
        mesh=mesh,
        in_specs=(
            P(("grp", "leaf"), None, None),
            P(("grp", "leaf"), None, None, None),
            P(("grp", "leaf"), None, None),
            P(("grp", "leaf"), None, None, None),
            P(("grp", "leaf"), None),
            P(("grp", "leaf"), None),
            P(("grp", "leaf"), None, None),
            P("grp", None, None),
        ),
        out_specs=(
            P(("grp", "leaf"), None, None),
            P(("grp", "leaf"), None, None),
            P("grp", None, None),
        ),
        check_vma=False,
    )
```

profile of v0, /device:TPU:1, one launch (start us, length us, event | category | flops | bytes accessed | tf_op | source)
XLA Modules:
  0.0 551.5 jit_solution(18114746774370927229)
XLA Ops:
  7.3 0.7 iota_compare_fusion
  8.0 0.5 copy-done
  8.4 2.8 fusion.5
  11.3 1.2 slice.142
  12.5 2.7 copy.75
  15.2 1.4 fusion.7
  16.6 1.0 copy-done.4
  17.7 23.5 %custom-call.29 = f32[2,128,128]{2,1,0:T(8,128)S(1)} custom-call(f32[2,128,128]{2,1,0:T(8,128)S(1)} %cholesky.204), custom_call_target="Cholesky" | custom-call | tf_op jit(solution)/shard_map/jit(cholesky)/cholesky | solution.py:41
  41.2 0.6 copy-done.6
  41.8 20.3 %custom-call.30 = f32[2,1,128,128]{2,3,1,0:T(8,128)} custom-call(f32[2,1,128,128]{3,2,1,0:T(8,128)S(1)} %select_bitcast_fusion.1), custom_call_target="InvertDiagBlocksLowerTriangular" | custom-call | tf_op jit(solution)/shard_map/jit(cholesky)/cholesky | solution.py:41
  62.0 1.0 cholesky.182
  63.9 0.7 copy-done.7
  64.6 0.7 cholesky.208
  65.2 24.9 %custom-call.31 = f32[2,128,128]{2,1,0:T(8,128)} custom-call(f32[2,128,128]{2,1,0:T(8,128)} %cholesky.208), custom_call_target="Cholesky" | custom-call | tf_op jit(solution)/shard_map/jit(cholesky)/cholesky | solution.py:41
  90.1 1.6 select_bitcast_fusion
  91.7 21.5 %custom-call.32 = f32[2,1,128,128]{2,3,1,0:T(8,128)} custom-call(f32[2,1,128,128]{3,2,1,0:T(8,128)} %get-tuple-element.27), custom_call_target="InvertDiagBlocksLowerTriangular" | custom-call | tf_op jit(solution)/shard_map/jit(cholesky)/cholesky | solution.py:41
  113.2 1.2 convolution_dynamic-update-slice_fusion
  114.4 1.0 convolution_subtract_fusion.4
  115.5 24.3 %custom-call.33 = f32[2,128,128]{2,1,0:T(8,128)S(1)} custom-call(f32[2,128,128]{2,1,0:T(8,128)} %convolution_subtract_fusion.4), custom_call_target="Cholesky" | custom-call | tf_op jit(solution)/shard_map/jit(cholesky)/cholesky | solution.py:41
  139.7 1.0 select_reduce_fusion.1
  141.0 1.1 select_select_fusion
  142.2 8.0 %while.1 = (s32[]{:T(128)}, f32[2,384,384]{2,1,0:T(8,128)S(1)}, s32[3,2]{0,1:T(2,128)S(1)}, f32[3,2,128,128]{3,2,0,1:T(8,128)}, s32[]{:T(128)}) while((s32[]{:T(128)}, f32[2,384,384]{2,1,0:T(8,128)S(1)}, s32[3,2]{0,1:T(2,128)S(1)}, f32[3,2,128,128]{3,2,0,1:T(8,128)}, s32[]{:T(128)}) %tuple.30), condition=%wide.while_cond, body=%wide.while_body.sunk | while | flops 2 | bytes 263277 | solution.py:29
  142.3 0.5 fusion.101
  142.8 2.1 bitcast_dynamic-update-slice_fusion.2
  144.9 0.5 fusion.101
  145.5 2.1 bitcast_dynamic-update-slice_fusion.2
  147.6 0.5 fusion.101
  148.1 2.1 bitcast_dynamic-update-slice_fusion.2
  150.2 59.9 %custom-call.34 = f32[2,3,128,128]{2,3,1,0:T(8,128)S(1)} custom-call(f32[2,3,128,128]{3,2,1,0:T(8,128)} %bitcast.158), custom_call_target="InvertDiagBlocksLowerTriangular" | custom-call | tf_op jit(solution)/shard_map/vmap(jit(_cho_solve))/triangular_solve | solution.py:29
  210.1 1.3 fusion.39
  211.4 1.2 convolution_subtract_fusion.6
  212.6 0.4 fusion.48
  213.0 1.3 convolution_subtract_fusion.3
  214.3 0.4 fusion.50
  215.0 0.4 convolution_subtract_fusion.5
  215.7 0.6 convolution_subtract_fusion.2
  216.6 1.5 convolution_subtract_fusion.1
  218.2 0.4 fusion.6
  218.8 1.4 convert_bitcast_fusion
  220.2 2.7 copy.52
  222.9 111.9 %all_to_all.5 = bf16[64,2,128,128]{3,2,1,0:T(8,128)(2,1)} all-to-all(bf16[64,2,128,128]{3,2,1,0:T(8,128)(2,1)S(1)} %copy.52), channel_id=1, replica_groups=mesh['grp'=8,'leaf'=64] {'leaf'}, dimensions={0} | all-to-all | bytes 8388608 | tf_op jit(solution)/shard_map/all_to_all | solution.py:93
  334.9 6.6 %fusion.11 = f32[1,128,128]{2,1,0:T(8,128)} fusion(bf16[64,2,128,128]{3,2,1,0:T(8,128)(2,1)} %all_to_all.5, bf16[1,128,128]{2,1,0:T(8,128)(2,1)S(1)} %copy-done.10), kind=kOutput, calls=%fused_computation.27 | convolution fusion | flops 1075838976 | bytes 4292608 | tf_op jit(solution)/shard_map/simk,sime->ike/dot_general | solution.py:97
  341.5 148.5 %all-reduce.3.cloned.1.call-done = f32[1,128,128]{2,1,0:T(8,128)} async-done(((f32[1,128,128]{2,1,0:T(8,128)}), f32[1,128,128]{2,1,0:T(8,128)}) %all-reduce.3.cloned.1.call-update) | async-done | bytes 65552 | tf_op jit(solution)/shard_map/psum | solution.py:99
  490.0 0.9 multiply_bitcast_fusion
  490.9 8.5 %collective-permute-start.2 = (f32[128,128]{1,0:T(8,128)S(1)}, f32[128,128]{1,0:T(8,128)S(1)}, u32[]{:S(2)}, u32[]{:S(2)}) collective-permute-start(f32[128,128]{1,0:T(8,128)S(1)} %multiply_bitcast_fusion), channel_id=1, source_target_pairs={{0,64},{64,128},{128,192},{192,256},{256,320},{320,384},{384,448},... | collective-permute-start | bytes 196616 | tf_op jit(solution)/shard_map/ppermute | solution.py:25
  499.4 1.1 collective-permute-done.2
  500.7 1.1 convolution_add_fusion.6
  501.8 4.3 collective-permute-start.3
  506.1 1.3 collective-permute-done.3
  507.6 1.1 convolution_add_fusion.5
  508.8 4.3 collective-permute-start.4
  513.0 1.0 slice.124
  514.0 1.3 collective-permute-start.1
  515.3 4.0 collective-permute-start
  519.9 2.5 collective-permute-start.5
  522.4 1.3 collective-permute-done.5
  524.2 4.3 collective-permute-start.6
  528.5 1.3 collective-permute-done.6
  530.3 4.3 collective-permute-start.7
  534.7 0.6 gather_fusion
  535.3 0.6 collective-permute-done.7
  536.4 4.3 collective-permute-start.8
  540.6 2.6 fusion.10
  543.5 0.9 fusion.14
  (60 shorter events, 5.2 us)
Async XLA Ops:
  7.2 1.3 copy-start
  7.2 482.8 %all-reduce.3.cloned.1.call-start = ((), (), s32[]{:S(2)}) async-start(), calls=%async_computation.1 | async-start | bytes 131072 | tf_op jit(solution)/shard_map/psum | solution.py:99
  11.3 3.9 copy-start.2
  16.6 1.0 copy-start.4
  17.7 45.4 %copy-start.5 = (f32[2,384,384]{2,1,0:T(8,128)S(1)}, f32[2,384,384]{2,1,0:T(8,128)}, u32[]{:S(2)}) copy-start(f32[2,384,384]{2,1,0:T(8,128)} %copy-done.4) | copy-start | bytes 3538948
  41.1 0.7 copy-start.6
  62.0 1.0 copy-start.9
  63.9 0.7 copy-start.7
  215.4 2.8 copy-start.8
  218.1 0.7 copy-start.11
  222.9 111.9 %copy-start.10 = (bf16[1,128,128]{2,1,0:T(8,128)(2,1)S(1)}, bf16[1,128,128]{2,1,0:T(8,128)(2,1)}, u32[]{:S(2)}) copy-start(bf16[1,128,128]{2,1,0:T(8,128)(2,1)} %param.14) | copy-start | bytes 98308
  334.8 165.6 %copy-start.1 = (f32[1,128,128]{2,1,0:T(8,128)S(1)}, f32[1,128,128]{2,1,0:T(8,128)}, u32[]{:S(2)}) copy-start(f32[1,128,128]{2,1,0:T(8,128)} %param.15) | copy-start | bytes 196612
  341.5 180.9 %copy-start.12 = (s32[2,1]{0,1:T(1,128)S(1)}, s32[2,1]{0,1:T(1,128)}, u32[]{:S(2)}) copy-start(s32[2,1]{0,1:T(1,128)} %param.12) | copy-start | bytes 28
  490.0 29.6 %copy-start.3 = (f32[1,128,128]{2,1,0:T(8,128)S(1)}, f32[1,128,128]{2,1,0:T(8,128)}, u32[]{:S(2)}) copy-start(f32[1,128,128]{2,1,0:T(8,128)} %all-reduce.3.cloned.1.call-done) | copy-start | bytes 196612
  490.9 9.6 %collective-permute-start.2 = (f32[128,128]{1,0:T(8,128)S(1)}, f32[128,128]{1,0:T(8,128)S(1)}, u32[]{:S(2)}, u32[]{:S(2)}) collective-permute-start(f32[128,128]{1,0:T(8,128)S(1)} %multiply_bitcast_fusion), channel_id=1, source_target_pairs={{0,64},{64,128},{128,192},{192,256},{256,320},{320,384},{384,448},... | collective-permute-start | bytes 196616 | tf_op jit(solution)/shard_map/ppermute | solution.py:25
  501.8 5.6 %collective-permute-start.3 = (f32[128,128]{1,0:T(8,128)S(1)}, f32[128,128]{1,0:T(8,128)S(1)}, u32[]{:S(2)}, u32[]{:S(2)}) collective-permute-start(f32[128,128]{1,0:T(8,128)S(1)} %convolution_add_fusion.6), channel_id=1, source_target_pairs={{0,64},{64,128},{128,192},{192,256},{256,320},{320,384},{384,448},... | collective-permute-start | bytes 196616 | tf_op jit(solution)/shard_map/ppermute | solution.py:25
  508.8 10.6 %collective-permute-start.4 = (f32[128,128]{1,0:T(8,128)S(1)}, f32[128,128]{1,0:T(8,128)S(1)}, u32[]{:S(2)}, u32[]{:S(2)}) collective-permute-start(f32[128,128]{1,0:T(8,128)S(1)} %convolution_add_fusion.5), channel_id=1, source_target_pairs={{0,64},{64,128},{128,192},{192,256},{256,320},{320,384},{384,448},... | collective-permute-start | bytes 196616 | tf_op jit(solution)/shard_map/ppermute | solution.py:25
  514.0 20.5 %collective-permute-start.1 = (bf16[2,512,128]{2,1,0:T(8,128)(2,1)S(1)}, bf16[2,512,128]{2,1,0:T(8,128)(2,1)S(1)}, u32[]{:S(2)}, u32[]{:S(2)}) collective-permute-start(bf16[2,512,128]{2,1,0:T(8,128)(2,1)S(1)} %slice.124), channel_id=1, source_target_pairs={{1,0},{2,1},{3,2},{4,3},{5,4},{6,5},{7,6},{8,7},{9,8},{10,9},{11,1... | collective-permute-start | bytes 786440 | tf_op jit(solution)/shard_map/ppermute | solution.py:17
  515.3 19.2 %collective-permute-start = (bf16[2,512,128]{2,1,0:T(8,128)(2,1)S(1)}, bf16[2,512,128]{2,1,0:T(8,128)(2,1)S(1)}, u32[]{:S(2)}, u32[]{:S(2)}) collective-permute-start(bf16[2,512,128]{2,1,0:T(8,128)(2,1)S(1)} %slice.124), channel_id=1, source_target_pairs={{0,1},{1,2},{2,3},{3,4},{4,5},{5,6},{6,7},{7,8},{8,9},{9,10},{10,1... | collective-permute-start | bytes 786440 | tf_op jit(solution)/shard_map/ppermute | solution.py:16
  519.9 3.8 collective-permute-start.5
  524.2 5.6 %collective-permute-start.6 = (f32[128,128]{1,0:T(8,128)S(1)}, f32[128,128]{1,0:T(8,128)S(1)}, u32[]{:S(2)}, u32[]{:S(2)}) collective-permute-start(f32[128,128]{1,0:T(8,128)S(1)} %convolution_add_fusion.3), channel_id=1, source_target_pairs={{0,64},{64,128},{128,192},{192,256},{256,320},{320,384},{384,448},... | collective-permute-start | bytes 196616 | tf_op jit(solution)/shard_map/ppermute | solution.py:25
  530.3 5.6 %collective-permute-start.7 = (f32[128,128]{1,0:T(8,128)S(1)}, f32[128,128]{1,0:T(8,128)S(1)}, u32[]{:S(2)}, u32[]{:S(2)}) collective-permute-start(f32[128,128]{1,0:T(8,128)S(1)} %convolution_add_fusion.2), channel_id=1, source_target_pairs={{0,64},{64,128},{128,192},{192,256},{256,320},{320,384},{384,448},... | collective-permute-start | bytes 196616 | tf_op jit(solution)/shard_map/ppermute | solution.py:25
  536.4 6.9 %collective-permute-start.8 = (f32[128,128]{1,0:T(8,128)S(1)}, f32[128,128]{1,0:T(8,128)S(1)}, u32[]{:S(2)}, u32[]{:S(2)}) collective-permute-start(f32[128,128]{1,0:T(8,128)S(1)} %convolution_add_fusion.1), channel_id=1, source_target_pairs={{0,64},{64,128},{128,192},{192,256},{256,320},{320,384},{384,448},... | collective-permute-start | bytes 196616 | tf_op jit(solution)/shard_map/ppermute | solution.py:25
Sparse Core Ops, SparseCore 0:
  341.6 148.2 all-reduce.2
where the time goes:
time: 561 us; the launch traced here: 552 us
  other arithmetic  182 us (32%)
  waiting for transfers between devices  154 us (27%)
  blocking collectives  112 us (20%)
  starting transfers between devices  37.6 us (7%)
  matrix products  30.6 us (5%)
  local copies, waits for them, and re-layouts  20.8 us (4%)
  between operations  14.8 us (3%)
    psum x1, waiting for transfers between devices, per_device(): group_root = lax.psum(parent, 'leaf')[0] / group_size  148 us
    another operation x13, other arithmetic, eliminate(): factor = jnp.linalg.cholesky(inner_block)  117 us
    all_to_all x1, blocking collectives, per_device(): lax.all_to_all(outgoing, 'leaf', split_axis=0, concat_axis=0, tiled=True)  112 us
    another operation x4, other arithmetic, solve_block(): return jax.scipy.linalg.cho_solve((factor, True), right_side)  61.8 us
    ppermute x7, starting transfers between devices, from_behind(): return lax.ppermute(value, axis, pairs)  32.3 us
  transfers between devices with their start and end apart: 10, of which 6 were waited for; matrix products, arithmetic and copies ran while one was open for 1% of the time, Pallas kernels for 0%

commit v1 on v0

v1 whole, which is shorter than its diff:
```python
import functools

import jax
import jax.numpy as jnp
from jax import lax
from jax.experimental import pallas as pl
from jax.experimental.pallas import tpu as pltpu
from jax.sharding import PartitionSpec as P

f32 = jnp.float32
bf16 = jnp.bfloat16
MESH = pl.DeviceIdType.MESH
VMEM = pl.BlockSpec(memory_space=pltpu.VMEM)
SMEM = pl.BlockSpec(memory_space=pltpu.SMEM)
ANY = pl.BlockSpec(memory_space=pl.ANY)
RING = 8
RANK = 128
HALF = 64
TILE = (8, 128)


def dot(a, b):
    return jnp.dot(a, b, preferred_element_type=f32)


def dot_t(a, b):
    return lax.dot_general(a, b, (((0,), (0,)), ((), ())), preferred_element_type=f32)


def dot_full(a, b):
    return jnp.dot(a, b, precision=lax.Precision.HIGHEST, preferred_element_type=f32)


def dot_t_full(a, b):
    return lax.dot_general(
        a, b, (((0,), (0,)), ((), ())), precision=lax.Precision.HIGHEST, preferred_element_type=f32
    )


def invert_pair(mats):
    lane = lax.broadcasted_iota(jnp.int32, TILE, 1)
    sub = lax.broadcasted_iota(jnp.int32, TILE, 0)
    lane_all = lax.broadcasted_iota(jnp.int32, (RANK, RANK), 1)
    steps = RANK // 8
    spread = lambda x: jnp.broadcast_to(x, TILE)
    ahead = [a[0:8] for a in mats]
    for s in range(steps):
        c0 = 8 * s
        inside = (lane >= c0) & (lane < c0 + 8)
        inside_all = (lane_all >= c0) & (lane_all < c0 + 8)
        last = s + 1 == steps
        strips, coming = [], []
        for a, strip in zip(mats, ahead):
            cols = [spread(strip[:, c0 + i : c0 + i + 1]) for i in range(8)]
            block = {(j, i): spread(cols[i][j : j + 1]) for i in range(8) for j in range(i, 8)}
            rows = [
                jnp.where(inside, jnp.where(lane == c0 + j, 1.0, 0.0), spread(strip[j : j + 1]))
                for j in range(8)
            ]
            if not last:
                below = a[c0 + 8 : c0 + 16]
                left = [spread(below[:, c0 + i : c0 + i + 1]) for i in range(8)]
                following = jnp.where(inside, 0.0, below)
            pivots, mult = [], {}
            for k in range(8):
                pivots.append(1.0 / block[k, k])
                for j in range(k + 1, 8):
                    for i in range(k + 1, j + 1):
                        block[j, i] = block[j, i] - (block[j, k] * block[i, k]) * pivots[k]
                    mult[j, k] = block[j, k] * pivots[k]
                for j in range(k + 1, 8):
                    rows[j] = rows[j] - mult[j, k] * rows[k]
                    if not last:
                        left[j] = left[j] - mult[j, k] * left[k]
                if not last:
                    following = following - left[k] * (rows[k] * pivots[k])
            if not last:
                coming.append(following)
            rows = [rows[k] * pivots[k] for k in range(8)]
            for k in range(7, 0, -1):
                for j in range(k):
                    rows[j] = rows[j] - mult[k, j] * rows[k]
            strip = rows[0]
            for j in range(1, 8):
                strip = jnp.where(sub == j, rows[j], strip)
            strips.append(strip)
        results = []
        for a, strip in zip(mats, strips):
            nothing = jnp.zeros_like(strip)
            placed = jnp.concatenate([strip if t == s else nothing for t in range(steps)], axis=0)
            a = jnp.where(inside_all, 0.0, a) - dot_full(a, placed)
            results.append(
                jnp.concatenate([strip if t == s else a[8 * t : 8 * t + 8] for t in range(steps)], axis=0)
            )
        mats, ahead = results, coming
    return mats


def form_reduced(leaves, blocks_ref, basis_ref, reduced):
    parts = basis_ref.shape[1] // RANK
    for l in range(leaves):
        basis = basis_ref[l]
        turned = dot(blocks_ref[l], basis).astype(bf16)
        reduced[l] = dot_t(turned, basis)
        for i in range(parts - 1):
            for j in range(i, parts - 1):
                si, sj = pl.ds(RANK * i, RANK), pl.ds(RANK * j, RANK)
                x = 0.5 * (reduced[l, si, sj] + reduced[l, sj, si].T)
                reduced[l, si, sj] = x
                if j > i:
                    reduced[l, sj, si] = x.T


def eliminate_block(leaves, k, parts, reduced):
    here = pl.ds(RANK * k, RANK)
    rest = pl.ds(RANK * (k + 1), RANK * (parts - 1 - k))
    inverses = invert_pair([reduced[l, here, here] for l in range(leaves)])
    for l in range(leaves):
        solved = dot_full(inverses[l], reduced[l, here, rest])
        reduced[l, rest, rest] = reduced[l, rest, rest] - dot_full(reduced[l, rest, here], solved)


def schur_kernel(near_list, blocks_ref, basis_ref, near_ref, halo, schur_ref, panels_ref, reduced):
    leaves, width = blocks_ref.shape[:2]
    parts = width // RANK
    skeleton = pl.ds(width - RANK, RANK)
    form_reduced(leaves, blocks_ref, basis_ref, reduced)
    for k in range(parts - 1):
        eliminate_block(leaves, k, parts, reduced)
    first = ((lax.axis_index("grp") * lax.axis_size("leaf") + lax.axis_index("leaf")) - 1) * leaves
    for l in range(leaves):
        schur = reduced[l, skeleton, skeleton]
        schur_ref[l] = schur
        place = near_list[l, 0] - first
        place = jnp.where(place < leaves, place, place - leaves)
        facing = dot_t(basis_ref[l, :, skeleton], near_ref[l, 0]).astype(bf16)
        panels_ref[l] = schur + dot(facing, halo[place])


class Places:
    def __init__(self):
        self.grp = lax.axis_index("grp")
        self.leaf = lax.axis_index("leaf")
        self.z = self.leaf // RING
        self.y = self.leaf % RING

    def on_z(self, z):
        return (self.grp, z * RING + self.y)

    def on_y(self, y):
        return (self.grp, self.z * RING + y)

    def on_grp(self, grp):
        return (grp, self.leaf)

    def on_leaf(self, step):
        n = lax.axis_size("leaf")
        return (self.grp, (self.leaf + step + n) % n)


def others(pos):
    return [(pos + o) % RING for o in range(1, RING)]


def greet(at, leaf_line):
    barrier = pltpu.get_barrier_semaphore()
    ids = [at.on_z(i) for i in others(at.z)] + [at.on_y(i) for i in others(at.y)]
    ids += [at.on_grp(i) for i in others(at.grp)]
    if leaf_line:
        ids += [at.on_leaf(1), at.on_leaf(-1)]
    for i in ids:
        pl.semaphore_signal(barrier, inc=1, device_id=i, device_id_type=MESH)
    pl.semaphore_wait(barrier, len(ids))


def remote(src, dst, send, recv, to):
    return pltpu.make_async_remote_copy(
        src_ref=src, dst_ref=dst, send_sem=send, recv_sem=recv, device_id=to, device_id_type=MESH
    )


def exchange(pos, to, src, dst, send, recv):
    copies = []
    for o in range(1, RING):
        i = (pos + o) % RING
        copy = remote(src(i), dst.at[pos], send.at[o], recv.at[o], to(i))
        copy.start()
        copies.append(copy)
    return copies


def wait_all(copies):
    for copy in copies:
        copy.wait()


def spread_kernel(kernel_ref, basis_ref, chain_ref, upper, lower, halo, chain, send_1, recv_1, send_2, recv_2, own):
    at = Places()
    leaves, width = basis_ref.shape[:2]
    skeleton = basis_ref.at[:, :, pl.ds(width - RANK, RANK)]
    top = kernel_ref.at[0, pl.ds(0, HALF)]
    bottom = kernel_ref.at[0, pl.ds(HALF, HALF)]
    mine = [
        pltpu.make_async_copy(top, upper.at[at.y, at.z], own.at[0]),
        pltpu.make_async_copy(bottom, lower.at[at.z, at.y], own.at[1]),
        pltpu.make_async_copy(chain_ref.at[0], chain.at[at.grp], own.at[2]),
    ]
    for copy in mine:
        copy.start()
    greet(at, True)
    first = exchange(at.z, at.on_z, lambda i: top, upper.at[at.y], send_1.at[0], recv_1.at[0])
    second = exchange(at.y, at.on_y, lambda i: bottom, lower.at[at.z], send_1.at[1], recv_1.at[1])
    third = exchange(at.grp, at.on_grp, lambda i: chain_ref.at[0], chain, send_1.at[2], recv_1.at[2])
    to_right = remote(skeleton, halo.at[pl.ds(0, leaves)], send_1.at[0, 0], recv_1.at[0, 0], at.on_leaf(1))
    to_left = remote(skeleton, halo.at[pl.ds(leaves, leaves)], send_1.at[1, 0], recv_1.at[1, 0], at.on_leaf(-1))
    to_right.start()
    to_left.start()
    wait_all(mine)
    wait_all(first)
    wait_all(second)
    for t in range(1, RING // 2 + 1):
        copies = []
        for h, (table, pos, to) in enumerate(((upper, at.y, at.on_y), (lower, at.z, at.on_z))):
            up = (pos - t + 1 + RING) % RING
            copies.append(remote(table.at[up], table.at[up], send_2.at[h, 0, t], recv_2.at[h, 0, t], to((pos + 1) % RING)))
            if t < RING // 2:
                down = (pos + t - 1) % RING
                copies.append(
                    remote(table.at[down], table.at[down], send_2.at[h, 1, t], recv_2.at[h, 1, t], to((pos + RING - 1) % RING))
                )
        for copy in copies:
            copy.start()
        wait_all(copies)
    wait_all(third)
    to_right.wait()
    to_left.wait()


def merge_kernel(
    adm, inverse, schur_ref, transfer_ref, upper, lower, chain_ref, parent_ref, top_ref,
    terms, shares, down_in, up_in, near_sum, far_in, local, slabs, slab_in, prefix, cross,
    send_c, recv_c, send_f, recv_f, send_r, recv_r,
):
    at = Places()
    leaves, entries = transfer_ref.shape[:2]
    greet(at, False)

    local[...] = jnp.zeros_like(local)
    lowered = [schur_ref[l].astype(bf16) for l in range(leaves)]

    for l in range(leaves):

        @pl.loop(0, entries // 4)
        def _(step, l=l):
            total = local[...]
            for i in range(4):
                a = step * 4 + i
                p = adm[l, a]
                pz, py = p // RING, p % RING
                lifted = dot(lowered[l], transfer_ref[l, a]).astype(bf16)
                kernel = jnp.concatenate([upper[py, pz], lower[pz, py]], axis=0)
                mixture = dot(kernel, lifted).astype(bf16)
                term = dot_t(lifted, mixture)
                terms[l * entries + a] = term.astype(bf16)
                total = total + term
            local[...] = total

    terms[leaves * entries] = jnp.zeros((RANK, RANK), bf16)

    @pl.loop(0, RING)
    def _(pz):
        for py in range(RING):
            p = pz * RING + py
            share = terms[inverse[0, p]].astype(f32)
            for l in range(1, leaves):
                share = share + terms[inverse[l, p]].astype(f32)
            share = share.astype(bf16)
            shares[0, pz, py] = share[:HALF]
            shares[1, py, pz] = share[HALF:]

    lines = ((at.z, at.on_z), (at.y, at.on_y))
    size = RING // 2

    def down_copy(h, t):
        pos, to = lines[h]
        src = shares.at[h, (pos - 5 + t + RING) % RING] if t == 1 else down_in.at[h, t - 2]
        return remote(src, down_in.at[h, t - 1], send_c.at[h, 0, t], recv_c.at[h, 0, t], to((pos + RING - 1) % RING))

    def up_copy(h, t):
        pos, to = lines[h]
        src = shares.at[h, (pos + 4 - t) % RING] if t == 1 else up_in.at[h, t - 2]
        return remote(src, up_in.at[h, t - 1], send_c.at[h, 1, t], recv_c.at[h, 1, t], to((pos + 1) % RING))

    def add_share(buffer, h, chunk):
        @pl.loop(0, RING)
        def _(i):
            buffer[i] = (buffer[i].astype(f32) + shares[h, chunk, i].astype(f32)).astype(bf16)

    down = [[None] * (size + 1) for _ in range(2)]
    up = [[None] * (size + 1) for _ in range(2)]
    for h in range(2):
        down[h][1] = down_copy(h, 1)
        down[h][1].start()
        up[h][1] = up_copy(h, 1)
        up[h][1].start()

    depth = RANK // RING
    r1 = exchange(
        at.z, at.on_z, lambda i: local.at[pl.ds(pl.multiple_of(i * depth, depth), depth)], slab_in.at[0],
        send_r.at[0], recv_r.at[0],
    )

    eye = (
        lax.broadcasted_iota(jnp.int32, (RANK, RANK), 0) == lax.broadcasted_iota(jnp.int32, (RANK, RANK), 1)
    ).astype(f32)
    running = jnp.zeros((RANK, RANK), f32)
    for j in range(RING - 1, -1, -1):
        if j < RING - 1:
            step_map = 0.8 * eye + 0.5 * chain_ref[j + 1]
            running = jnp.where(j < at.grp, dot_full(step_map, running), 0.0)
        running = jnp.where(j == at.grp, eye, running)
        prefix[j] = running

    def chain_step(t):
        for h in range(2):
            pos, _ = lines[h]
            down[h][t - 1].wait()
            add_share(down_in.at[h, t - 2], h, (pos - 5 + t + RING) % RING)
            down[h][t] = down_copy(h, t)
            down[h][t].start()
            up[h][t - 1].wait()
            if t < size:
                add_share(up_in.at[h, t - 2], h, (pos + 4 - t) % RING)
                up[h][t] = up_copy(h, t)
                up[h][t].start()

    def gathered(stage, pos, mine):
        total = mine
        for o in range(1, RING):
            total = total + slab_in[stage, (pos + o) % RING]
        return total

    chain_step(2)
    wait_all(r1)
    slabs[0] = gathered(0, at.z, local[pl.ds(pl.multiple_of(at.z * depth, depth), depth)])
    r2 = exchange(at.y, at.on_y, lambda i: slabs.at[0], slab_in.at[1], send_r.at[1], recv_r.at[1])
    chain_step(3)
    wait_all(r2)
    slabs[1] = gathered(1, at.y, slabs[0]) * (1.0 / (RING * RING))
    r3 = exchange(at.grp, at.on_grp, lambda i: slabs.at[1], slab_in.at[2], send_r.at[2], recv_r.at[2])
    chain_step(4)
    wait_all(r3)
    slab_in[2, at.grp] = slabs[1]
    mine = pl.ds(pl.multiple_of(at.z * depth, depth), depth)
    rows = jnp.concatenate([prefix[j, mine] for j in range(RING)], axis=0)
    mapped = jnp.concatenate([dot_full(slab_in[2, j], prefix[j]) for j in range(RING)], axis=0)
    cross[...] = dot_t_full(rows, mapped)
    my_rows = pl.ds(pl.multiple_of(at.y * depth, depth), depth)
    r4 = exchange(at.z, at.on_z, lambda i: cross.at[my_rows], slab_in.at[3], send_r.at[3], recv_r.at[3])

    far = []
    for h in range(2):
        pos, _ = lines[h]
        down[h][size].wait()

        @pl.loop(0, RING)
        def _(i, h=h, pos=pos):
            near_sum[h, i] = (
                down_in[h, size - 1, i].astype(f32) + up_in[h, size - 2, i].astype(f32) + shares[h, pos, i].astype(f32)
            ).astype(bf16)

        other, to = lines[1 - h]
        far += exchange(other, to, lambda i, h=h: near_sum.at[h, i], far_in.at[h], send_f.at[h], recv_f.at[h])
    wait_all(r4)
    slabs[2] = gathered(3, at.z, cross[my_rows])
    r5 = exchange(at.y, at.on_y, lambda i: slabs.at[2], slab_in.at[4], send_r.at[4], recv_r.at[4])
    wait_all(far)
    for h in range(2):
        other, _ = lines[1 - h]
        total = near_sum[h, other].astype(f32)
        for o in range(1, RING):
            total = total + far_in[h, (other + o) % RING].astype(f32)
        parent_ref[0, pl.ds(h * HALF, HALF)] = total
    wait_all(r5)
    slab_in[4, at.y] = slabs[2]
    for i in range(RING):
        top_ref[0, pl.ds(i * depth, depth)] = slab_in[4, i]


def per_device(self_blocks, near_blocks, leaf_basis, transfer, near_list, adm_list, parent_kernel, chain_coupling):
    leaves, width = leaf_basis.shape[:2]
    entries = transfer.shape[1]
    depth = RANK // RING
    sems = pltpu.SemaphoreType.DMA
    shape = jax.ShapeDtypeStruct
    upper, lower, halo, chain = pl.pallas_call(
        spread_kernel,
        out_shape=(
            shape((RING, RING, HALF, RANK), bf16),
            shape((RING, RING, HALF, RANK), bf16),
            shape((2 * leaves, width, RANK), bf16),
            shape((RING, RANK, RANK), f32),
        ),
        in_specs=[ANY, ANY, ANY],
        out_specs=(ANY, ANY, ANY, ANY),
        scratch_shapes=[
            sems((3, RING)), sems((3, RING)), sems((2, 2, RING)), sems((2, 2, RING)), sems((3,)),
        ],
        compiler_params=pltpu.CompilerParams(collective_id=0, has_side_effects=True),
    )(parent_kernel, leaf_basis, chain_coupling)
    schur, panels = pl.pallas_call(
        schur_kernel,
        out_shape=(shape((leaves, RANK, RANK), f32), shape((leaves, RANK, RANK), f32)),
        in_specs=[SMEM, VMEM, VMEM, VMEM, VMEM],
        out_specs=(VMEM, VMEM),
        scratch_shapes=[pltpu.VMEM((leaves, width, width), f32)],
        compiler_params=pltpu.CompilerParams(vmem_limit_bytes=40 * 2**20),
    )(near_list, self_blocks, leaf_basis, near_blocks, halo)
    order = jnp.arange(leaves * entries, dtype=jnp.int32).reshape(leaves, entries, 1)
    names = adm_list[:, :, None] == jnp.arange(RING * RING, dtype=jnp.int32)[None, None, :]
    inverse = jnp.min(jnp.where(names, order, leaves * entries), axis=1)
    parent, top = pl.pallas_call(
        merge_kernel,
        out_shape=(shape((1, RANK, RANK), f32), shape((1, RANK, RANK), f32)),
        in_specs=[SMEM, SMEM, VMEM, VMEM, VMEM, VMEM, VMEM],
        out_specs=(VMEM, VMEM),
        scratch_shapes=[
            pltpu.VMEM((leaves * entries + 1, RANK, RANK), bf16),
            pltpu.VMEM((2, RING, RING, HALF, RANK), bf16),
            pltpu.VMEM((2, RING // 2, RING, HALF, RANK), bf16),
            pltpu.VMEM((2, RING // 2 - 1, RING, HALF, RANK), bf16),
            pltpu.VMEM((2, RING, HALF, RANK), bf16),
            pltpu.VMEM((2, RING, HALF, RANK), bf16),
            pltpu.VMEM((RANK, RANK), f32),
            pltpu.VMEM((3, depth, RANK), f32),
            pltpu.VMEM((5, RING, depth, RANK), f32),
            pltpu.VMEM((RING, RANK, RANK), f32),
            pltpu.VMEM((RANK, RANK), f32),
            sems((2, 2, RING)), sems((2, 2, RING)),
            sems((2, RING)), sems((2, RING)),
            sems((5, RING)), sems((5, RING)),
        ],
        compiler_params=pltpu.CompilerParams(
            collective_id=1, has_side_effects=True, vmem_limit_bytes=40 * 2**20
        ),
    )(adm_list, inverse, schur, transfer, upper, lower, chain)
    return panels, parent, top


def solution(mesh):
    lead = P(("grp", "leaf"))
    return jax.shard_map(
        per_device,
        mesh=mesh,
        in_specs=(lead, lead, lead, lead, lead, lead, lead, P("grp")),
        out_specs=(lead, lead, P("grp")),
        check_vma=False,
    )
```

time: 561 us -> 115 us (0.20)
  the two profiles are of different devices: /device:TPU:1 before, /device:TPU:56 now
where the time goes in v1:
time: 115 us; the launch traced here: 114 us
  Pallas kernels  107 us (93%)
  local copies, waits for them, and re-layouts  6.19 us (5%)
    pallas_call x1, Pallas kernels, per_device(): pl.pallas_call(spread_kernel, out_shape=(shape((RING, RING, HALF, RANK),...  43.2 us
    pallas_call x1, Pallas kernels, per_device(): pl.pallas_call(merge_kernel, out_shape=(shape((1, RANK, RANK), f32), shap...  42.4 us
    pallas_call x1, Pallas kernels, per_device(): pl.pallas_call(schur_kernel, out_shape=(shape((leaves, RANK, RANK), f32),...  21.2 us
    unnamed x23, local copies, waits for them, and re-layouts  6.19 us

profile of v1, /device:TPU:56, one launch (start us, length us, event | category | flops | bytes accessed | tf_op | source)
XLA Modules:
  0.0 113.8 jit_solution(11558577644585579826)
XLA Ops:
  0.6 0.0 copy-start
  0.6 43.2 %shard_map.103 = (bf16[8,8,64,128]{3,2,1,0:T(8,128)(2,1)}, bf16[8,8,64,128]{3,2,1,0:T(8,128)(2,1)}, bf16[4,512,128]{2,1,0:T(8,128)(2,1)}, f32[8,128,128]{2,1,0:T(8,128)}) custom-call(bf16[1,128,128]{2,1,0:T(8,128)(2,1)} %kernel_ref.1, bf16[2,512,512]{2,1,0:T(8,128)(2,1)} %basis_ref.3, f32[1,128,128]{2,1,0:T(8,128)} %chain_ref.1), custom_call_target="tpu_custom_call" | custom-call | tf_op jit(solution)/shard_map/pallas_call | solution.py:396
  43.9 0.0 copy-start.9
  43.9 0.6 copy-done.9
  44.5 0.1 copy.12.near_list
  44.6 0.0 copy-done
  44.6 0.0 copy-start.4
  44.6 1.2 %copy-done.4 = bf16[2,512,512]{2,1,0:T(8,128)(2,1)S(1)} copy-done((bf16[2,512,512]{2,1,0:T(8,128)(2,1)S(1)}, bf16[2,512,512]{2,1,0:T(8,128)(2,1)}, u32[]{:S(2)}) %copy-start.4) | copy-done | bytes 1048600
  45.9 0.0 copy-start.5
  45.9 1.2 %copy-done.5 = bf16[2,1,512,512]{3,2,1,0:T(8,128)(2,1)S(1)} copy-done((bf16[2,1,512,512]{3,2,1,0:T(8,128)(2,1)S(1)}, bf16[2,1,512,512]{3,2,1,0:T(8,128)(2,1)}, u32[]{:S(2)}) %copy-start.5) | copy-done | bytes 1048600
  47.1 0.0 copy-start.7
  47.1 1.0 copy-done.7
  48.1 0.0 copy-start.1
  48.1 0.0 copy-start.2
  48.1 0.0 copy-start.3
  48.1 0.0 copy-start.6
  48.1 21.2 %shard_map.104 = (f32[2,128,128]{2,1,0:T(8,128)S(1)}, f32[2,128,128]{2,1,0:T(8,128)}) custom-call(s32[2,1]{1,0:T(2,128)S(1)} %copy.12.near_list, bf16[2,512,512]{2,1,0:T(8,128)(2,1)S(1)} %copy-done.4, bf16[2,512,512]{2,1,0:T(8,128)(2,1)S(1)} %copy-done, bf16[2,1,512,512]{3,2,1,0:T(8,128)(2,1)S(1)} %copy-done.5, bf16[4,512,128]{2,1,0:T(8,128)(2,1)S(1)} %copy-done.7), custom_call_target="tpu_custom_call" | custom-call | tf_op jit(solution)/shard_map/pallas_call | solution.py:411
  69.3 0.0 copy-start.8
  69.4 0.7 copy-done.8
  70.0 0.1 select_reduce_fusion.inverse
  70.1 0.0 copy-done.1
  70.1 0.0 copy-done.2
  70.1 0.0 copy-done.3
  70.1 0.0 copy-done.6
  70.2 42.4 %shard_map.105 = (f32[1,128,128]{2,1,0:T(8,128)S(1)}, f32[1,128,128]{2,1,0:T(8,128)S(1)}) custom-call(s32[2,16]{1,0:T(2,128)S(1)} %copy-done.8, s32[2,64]{1,0:T(2,128)S(1)} %select_reduce_fusion.inverse, f32[2,128,128]{2,1,0:T(8,128)S(1)} %get-tuple-element.13.schur_ref, bf16[2,16,128,128]{3,2,1,0:T(8,128)(2,1)S(1)} %copy-done.1, ...), custom_call_target="tpu_custom_call" | custom-call | tf_op jit(solution)/shard_map/pallas_call | solution.py:422
  112.5 0.6 copy.15
  113.2 0.6 copy.16
  (1 shorter events, 0.0 us)
Async XLA Ops:
  0.6 44.0 %copy-start = (bf16[2,512,512]{2,1,0:T(8,128)(2,1)S(1)}, bf16[2,512,512]{2,1,0:T(8,128)(2,1)}, u32[]{:S(2)}) copy-start(bf16[2,512,512]{2,1,0:T(8,128)(2,1)} %basis_ref.3) | copy-start | bytes 3145732
  43.9 0.7 copy-start.9
  44.6 1.2 %copy-start.4 = (bf16[2,512,512]{2,1,0:T(8,128)(2,1)S(1)}, bf16[2,512,512]{2,1,0:T(8,128)(2,1)}, u32[]{:S(2)}) copy-start(bf16[2,512,512]{2,1,0:T(8,128)(2,1)} %blocks_ref.1) | copy-start | bytes 3145732
  45.9 1.2 %copy-start.5 = (bf16[2,1,512,512]{3,2,1,0:T(8,128)(2,1)S(1)}, bf16[2,1,512,512]{3,2,1,0:T(8,128)(2,1)}, u32[]{:S(2)}) copy-start(bf16[2,1,512,512]{3,2,1,0:T(8,128)(2,1)} %near_ref.1) | copy-start | bytes 3145732
  47.1 1.0 copy-start.7
  48.1 22.0 %copy-start.1 = (bf16[2,16,128,128]{3,2,1,0:T(8,128)(2,1)S(1)}, bf16[2,16,128,128]{3,2,1,0:T(8,128)(2,1)}, u32[]{:S(2)}) copy-start(bf16[2,16,128,128]{3,2,1,0:T(8,128)(2,1)} %transfer_ref.1) | copy-start | bytes 3145732
  48.1 22.0 %copy-start.2 = (bf16[8,8,64,128]{3,2,1,0:T(8,128)(2,1)S(1)}, bf16[8,8,64,128]{3,2,1,0:T(8,128)(2,1)}, u32[]{:S(2)}) copy-start(bf16[8,8,64,128]{3,2,1,0:T(8,128)(2,1)} %get-tuple-element.14.upper) | copy-start | bytes 3145732
  48.1 22.0 %copy-start.3 = (bf16[8,8,64,128]{3,2,1,0:T(8,128)(2,1)S(1)}, bf16[8,8,64,128]{3,2,1,0:T(8,128)(2,1)}, u32[]{:S(2)}) copy-start(bf16[8,8,64,128]{3,2,1,0:T(8,128)(2,1)} %get-tuple-element.15.lower) | copy-start | bytes 3145732
  48.1 22.0 %copy-start.6 = (f32[8,128,128]{2,1,0:T(8,128)S(1)}, f32[8,128,128]{2,1,0:T(8,128)}, u32[]{:S(2)}) copy-start(f32[8,128,128]{2,1,0:T(8,128)} %get-tuple-element.16.chain_ref) | copy-start | bytes 1572868
  69.3 0.7 copy-start.8

commit v2 on v0

v2 whole, which is shorter than its diff:
```python
import functools

import jax
import jax.numpy as jnp
from jax import lax
from jax.experimental import pallas as pl
from jax.experimental.pallas import tpu as pltpu
from jax.sharding import PartitionSpec as P

f32 = jnp.float32
bf16 = jnp.bfloat16
MESH = pl.DeviceIdType.MESH
VMEM = pl.BlockSpec(memory_space=pltpu.VMEM)
SMEM = pl.BlockSpec(memory_space=pltpu.SMEM)
ANY = pl.BlockSpec(memory_space=pl.ANY)
RING = 8
RANK = 128
HALF = 64
TILE = (8, 128)


def dot(a, b):
    return jnp.dot(a, b, preferred_element_type=f32)


def dot_t(a, b):
    return lax.dot_general(a, b, (((0,), (0,)), ((), ())), preferred_element_type=f32)


def dot_full(a, b):
    return jnp.dot(a, b, precision=lax.Precision.HIGHEST, preferred_element_type=f32)


def dot_t_full(a, b):
    return lax.dot_general(
        a, b, (((0,), (0,)), ((), ())), precision=lax.Precision.HIGHEST, preferred_element_type=f32
    )


def factor_strip(strip, below, c0):
    shape = strip.shape
    lane = lax.broadcasted_iota(jnp.int32, shape, 2)
    sub = lax.broadcasted_iota(jnp.int32, shape, 1)
    inside = (lane >= c0) & (lane < c0 + 8)
    column = lambda x, i: jnp.broadcast_to(x[:, :, c0 + i : c0 + i + 1], shape)
    row = lambda x, j: jnp.broadcast_to(x[:, j : j + 1], shape)
    columns = [column(strip, i) for i in range(8)]
    block = [jnp.stack([row(columns[i], j) for j in range(i, 8)], axis=0) for i in range(8)]
    rows = jnp.stack(
        [jnp.where(inside, jnp.where(lane == c0 + j, 1.0, 0.0), row(strip, j)) for j in range(8)], axis=0
    )
    following = None
    if below is not None:
        left = jnp.stack([column(below, i) for i in range(8)], axis=0)
        following = jnp.where(inside, 0.0, below)
    mult, scaled = [], []
    for k in range(8):
        pivot = 1.0 / block[k][0]
        for i in range(k + 1, 8):
            block[i] = block[i] - (block[k][i - k :] * block[k][i - k]) * pivot
        scaled.append(rows[0] * pivot)
        if below is not None:
            following = following - left[0] * scaled[k]
        if k < 7:
            mult.append(block[k][1:] * pivot)
            rows = rows[1:] - mult[k] * rows[0]
            if below is not None:
                left = left[1:] - mult[k] * left[0]
    rows = jnp.stack(scaled, axis=0)
    result = None
    for k in range(7, -1, -1):
        result = rows[k] if result is None else jnp.where(sub == k, rows[k], result)
        if k > 0:
            rows = rows[:k] - jnp.stack([mult[j][k - j - 1] for j in range(k)], axis=0) * rows[k]
    return result, following


def invert(mats, between):
    leaves = mats.shape[0]
    lane = lax.broadcasted_iota(jnp.int32, (RANK, RANK), 1)
    steps = RANK // 8
    ahead = mats[:, 0:8]
    for s in range(steps):
        c0 = 8 * s
        strip, ahead = factor_strip(ahead, mats[:, c0 + 8 : c0 + 16] if s + 1 < steps else None, c0)
        inside = (lane >= c0) & (lane < c0 + 8)
        results = []
        for l in range(leaves):
            nothing = jnp.zeros(TILE, f32)
            placed = jnp.concatenate([strip[l] if t == s else nothing for t in range(steps)], axis=0)
            rest = jnp.where(inside, 0.0, mats[l]) - dot_full(mats[l], placed)
            results.append(
                jnp.concatenate([strip[l] if t == s else rest[8 * t : 8 * t + 8] for t in range(steps)], axis=0)
            )
        mats = jnp.stack(results, axis=0)
        between(s)
    return mats


def form_reduced(l, parts, blocks, basis, reduced):
    turned = dot(blocks[l], basis[l]).astype(bf16)
    reduced[l] = dot_t(turned, basis[l])
    for i in range(parts - 1):
        for j in range(i, parts - 1):
            si, sj = pl.ds(RANK * i, RANK), pl.ds(RANK * j, RANK)
            x = 0.5 * (reduced[l, si, sj] + reduced[l, sj, si].T)
            reduced[l, si, sj] = x
            if j > i:
                reduced[l, sj, si] = x.T


def eliminate(leaves, parts, reduced, inverses, between):
    @pl.loop(0, parts - 1)
    def _(k):
        here = pl.ds(pl.multiple_of(k * RANK, RANK), RANK)
        inverses[...] = invert(reduced[:, here, here], functools.partial(between, k))
        for known in range(parts - 1):

            @pl.when(k == known)
            def _(known=known):
                here = pl.ds(RANK * known, RANK)
                rest = pl.ds(RANK * (known + 1), RANK * (parts - 1 - known))
                for l in range(leaves):
                    solved = dot_full(inverses[l], reduced[l, here, rest])
                    reduced[l, rest, rest] = reduced[l, rest, rest] - dot_full(reduced[l, rest, here], solved)


class Places:
    def __init__(self):
        self.grp = lax.axis_index("grp")
        self.leaf = lax.axis_index("leaf")
        self.z = self.leaf // RING
        self.y = self.leaf % RING

    def on_z(self, z):
        return (self.grp, z * RING + self.y)

    def on_y(self, y):
        return (self.grp, self.z * RING + y)

    def on_grp(self, grp):
        return (grp, self.leaf)

    def on_leaf(self, step):
        n = lax.axis_size("leaf")
        return (self.grp, (self.leaf + step + n) % n)


def others(pos):
    return [(pos + o) % RING for o in range(1, RING)]


def partners(at):
    ids = [at.on_z(i) for i in others(at.z)] + [at.on_y(i) for i in others(at.y)]
    return ids + [at.on_grp(i) for i in others(at.grp)] + [at.on_leaf(1), at.on_leaf(-1)]


def greet(at):
    for i in partners(at):
        pl.semaphore_signal(pltpu.get_barrier_semaphore(), inc=1, device_id=i, device_id_type=MESH)


def await_greetings(at):
    pl.semaphore_wait(pltpu.get_barrier_semaphore(), len(partners(at)))


def remote(src, dst, send, recv, to):
    return pltpu.make_async_remote_copy(
        src_ref=src, dst_ref=dst, send_sem=send, recv_sem=recv, device_id=to, device_id_type=MESH
    )


def exchange(pos, to, src, dst, send, recv):
    copies = []
    for o in range(1, RING):
        i = (pos + o) % RING
        copy = remote(src(i), dst.at[pos], send.at[o], recv.at[o], to(i))
        copy.start()
        copies.append(copy)
    return copies


def wait_all(copies):
    for copy in copies:
        copy.wait()


SIZE = RING // 2
PIECES = 2
DEPTH = RANK // RING
GATHER_AT = {(0, 3): 1, (0, 15): 2, (1, 13): 3, (2, 9): 4}


def kernel_body(
    near_list, adm, inverse, blocks_hbm, near_hbm, basis_hbm, transfer_hbm, kernel_hbm, chain_hbm,
    panels_ref, parent_ref, top_ref,
    blocks, near, basis, transfer, upper, lower, halo, maps, reduced, inverses, lifted, terms, shares,
    down_in, up_in, near_sum, far_in, local, local_in, prefix, cross, slabs, slab_in,
    load_sem, send_1, recv_1, send_2, recv_2, send_c, recv_c, send_f, recv_f, send_g, recv_g, send_r, recv_r,
):
    at = Places()
    leaves, width = basis.shape[:2]
    entries = transfer.shape[1]
    parts = width // RANK
    skeleton = pl.ds(width - RANK, RANK)
    lines = ((at.z, at.on_z), (at.y, at.on_y))

    top = kernel_hbm.at[0, pl.ds(0, HALF)]
    bottom = kernel_hbm.at[0, pl.ds(HALF, HALF)]
    loads = []
    for l in range(leaves):
        loads += [(basis_hbm.at[l], basis.at[l]), (blocks_hbm.at[l], blocks.at[l])]
    loads += [(near_hbm, near), (transfer_hbm, transfer)]
    loads += [(top, upper.at[at.y, at.z]), (bottom, lower.at[at.z, at.y]), (chain_hbm.at[0], maps.at[at.grp])]
    loads = [pltpu.make_async_copy(src, dst, load_sem.at[i]) for i, (src, dst) in enumerate(loads)]
    for load in loads:
        load.start()
    greet(at)

    for l in range(leaves):
        loads[2 * l].wait()
        loads[2 * l + 1].wait()
        form_reduced(l, parts, blocks, basis, reduced)
        if l == 0:
            await_greetings(at)
            exchange(at.z, at.on_z, lambda i: top, upper.at[at.y], send_1.at[0], recv_1.at[0])
            exchange(at.y, at.on_y, lambda i: bottom, lower.at[at.z], send_1.at[1], recv_1.at[1])
            exchange(at.grp, at.on_grp, lambda i: chain_hbm.at[0], maps, send_1.at[2], recv_1.at[2])

    def gather_copies(t):
        copies = []
        for h, (table, pos, to) in enumerate(((upper, at.y, at.on_y), (lower, at.z, at.on_z))):
            chunk = (pos - t + 1 + RING) % RING
            copies.append(
                remote(table.at[chunk], table.at[chunk], send_2.at[h, 0, t], recv_2.at[h, 0, t], to((pos + 1) % RING))
            )
            if t < SIZE:
                chunk = (pos + t - 1) % RING
                copies.append(
                    remote(
                        table.at[chunk], table.at[chunk], send_2.at[h, 1, t], recv_2.at[h, 1, t],
                        to((pos + RING - 1) % RING),
                    )
                )
        return copies

    def halo_copies():
        source = basis.at[:, :, skeleton]
        return [
            remote(source, halo.at[pl.ds(0, leaves)], send_1.at[0, 0], recv_1.at[0, 0], at.on_leaf(1)),
            remote(source, halo.at[pl.ds(leaves, leaves)], send_1.at[1, 0], recv_1.at[1, 0], at.on_leaf(-1)),
        ]

    def first_copies():
        return [
            remote(top, upper.at[at.y, at.z], send_1.at[0, o], recv_1.at[0, o], at.on_z((at.z + o) % RING))
            for o in range(1, RING)
        ] + [
            remote(bottom, lower.at[at.z, at.y], send_1.at[1, o], recv_1.at[1, o], at.on_y((at.y + o) % RING))
            for o in range(1, RING)
        ]

    def between(k, s):
        for (block, step), t in GATHER_AT.items():
            if s == step:

                @pl.when(k == block)
                def _(t=t):
                    if t == 1:
                        loads[-3].wait()
                        loads[-2].wait()
                        wait_all(first_copies())
                    else:
                        wait_all(gather_copies(t - 1))
                    for copy in gather_copies(t):
                        copy.start()
                    if t == SIZE:
                        for copy in halo_copies():
                            copy.start()

    eliminate(leaves, parts, reduced, inverses, between)

    loads[2 * leaves + 1].wait()
    group = 8
    for l in range(leaves):
        lowered = reduced[l, skeleton, skeleton].astype(bf16)

        @pl.loop(0, entries // group)
        def _(step, l=l, lowered=lowered):
            for i in range(group):
                a = step * group + i
                lifted[l * entries + a] = dot(lowered, transfer[l, a]).astype(bf16)

    wait_all(gather_copies(SIZE))
    local[...] = jnp.zeros_like(local)

    for l in range(leaves):

        @pl.loop(0, entries // group)
        def _(step, l=l):
            total = None
            for i in range(group):
                a = step * group + i
                p = adm[l, a]
                pz, py = p // RING, p % RING
                panel = lifted[l * entries + a]
                kernel = jnp.concatenate([upper[py, pz], lower[pz, py]], axis=0)
                mixture = dot(kernel, panel).astype(bf16)
                term = dot_t(panel, mixture)
                terms[l * entries + a] = term.astype(bf16)
                total = term if total is None else total + term
            local[...] += total

    terms[leaves * entries] = jnp.zeros((RANK, RANK), bf16)
    local_in[at.grp] = local[...].astype(bf16)
    by_grp = exchange(at.grp, at.on_grp, lambda i: local_in.at[at.grp], local_in, send_g, recv_g)

    @pl.loop(0, RING)
    def _(pz):
        for py in range(RING):
            p = pz * RING + py
            share = terms[inverse[0, p]].astype(f32)
            for l in range(1, leaves):
                share = share + terms[inverse[l, p]].astype(f32)
            share = share.astype(bf16)
            shares[0, pz, py] = share[:HALF]
            shares[1, py, pz] = share[HALF:]

    span = RING // PIECES

    def chain_copy(h, up, t, u):
        pos, to = lines[h]
        piece = pl.ds(u * span, span)
        buffer = (down_in, up_in)[up]
        chunk = (pos + 4 - t + RING) % RING if up else (pos - 5 + t + RING) % RING
        src = shares.at[h, chunk, piece] if t == 1 else buffer.at[h, t - 2, piece]
        target = (pos + 1) % RING if up else (pos + RING - 1) % RING
        return remote(src, buffer.at[h, t - 1, piece], send_c.at[h, up, t, u], recv_c.at[h, up, t, u], to(target))

    def chain_step(t):
        for u in range(PIECES):
            for h in range(2):
                pos, _ = lines[h]
                for up in range(2):
                    if t > 1:
                        chain_copy(h, up, t - 1, u).wait_recv()
                    if up and t == SIZE:
                        continue
                    if t > 1:
                        piece = pl.ds(u * span, span)
                        buffer = (down_in, up_in)[up]
                        chunk = (pos + 4 - t + RING) % RING if up else (pos - 5 + t + RING) % RING
                        mine = shares[h, chunk, piece].astype(f32)
                        buffer[h, t - 2, piece] = (buffer[h, t - 2, piece].astype(f32) + mine).astype(bf16)
                    chain_copy(h, up, t, u).start()

    chain_step(1)

    wait_all(
        [
            remote(chain_hbm.at[0], maps.at[at.grp], send_1.at[2, o], recv_1.at[2, o], at.on_grp((at.grp + o) % RING))
            for o in range(1, RING)
        ]
    )
    loads[-1].wait()
    eye = (
        lax.broadcasted_iota(jnp.int32, (RANK, RANK), 0) == lax.broadcasted_iota(jnp.int32, (RANK, RANK), 1)
    ).astype(f32)
    running = jnp.zeros((RANK, RANK), f32)
    for j in range(RING - 1, -1, -1):
        if j < RING - 1:
            step_map = 0.8 * eye + 0.5 * maps[j + 1]
            running = jnp.where(j < at.grp, dot_full(step_map, running), 0.0)
        running = jnp.where(j == at.grp, eye, running)
        high = running.astype(bf16)
        prefix[0, pl.ds(j * RANK, RANK)] = high
        prefix[1, pl.ds(j * RANK, RANK)] = (running - high.astype(f32)).astype(bf16)

    chain_step(2)

    wait_all(by_grp)
    mapped = jnp.concatenate(
        [
            dot(local_in[j], prefix[0, pl.ds(j * RANK, RANK)]) + dot(local_in[j], prefix[1, pl.ds(j * RANK, RANK)])
            for j in range(RING)
        ],
        axis=0,
    )
    high = mapped.astype(bf16)
    low = (mapped - high.astype(f32)).astype(bf16)
    cross[...] = (dot_t(prefix[0], high) + (dot_t(prefix[1], high) + dot_t(prefix[0], low))) * (1.0 / (RING * RING))

    slab = lambda i: pl.ds(pl.multiple_of(i * DEPTH, DEPTH), DEPTH)

    def gathered(stage, pos, mine):
        total = mine
        for o in range(1, RING):
            total = total + slab_in[stage, (pos + o) % RING]
        return total

    by_z = exchange(at.z, at.on_z, lambda i: cross.at[slab(i)], slab_in.at[0], send_r.at[0], recv_r.at[0])

    for copy in halo_copies():
        copy.wait()
    loads[2 * leaves].wait()
    first = ((at.grp * lax.axis_size("leaf") + at.leaf) - 1) * leaves
    for l in range(leaves):
        place = near_list[l, 0] - first
        place = jnp.clip(jnp.where(place < leaves, place, place - leaves), 0, 2 * leaves - 1)
        facing = dot_t(basis[l, :, skeleton], near[l, 0]).astype(bf16)
        panels_ref[l] = reduced[l, skeleton, skeleton] + dot(facing, halo[place])

    chain_step(3)
    wait_all(by_z)
    slabs[0] = gathered(0, at.z, cross[slab(at.z)])
    by_y = exchange(at.y, at.on_y, lambda i: slabs.at[0], slab_in.at[1], send_r.at[1], recv_r.at[1])
    chain_step(4)
    wait_all(by_y)
    slabs[1] = gathered(1, at.y, slabs[0])
    again = exchange(at.z, at.on_z, lambda i: slabs.at[1], slab_in.at[2], send_r.at[2], recv_r.at[2])

    far = []
    for h in range(2):
        pos, _ = lines[h]
        for u in range(PIECES):
            chain_copy(h, 0, SIZE, u).wait_recv()
        near_sum[h] = (
            down_in[h, SIZE - 1].astype(f32) + up_in[h, SIZE - 2].astype(f32) + shares[h, pos].astype(f32)
        ).astype(bf16)
        other, to = lines[1 - h]
        far += exchange(other, to, lambda i, h=h: near_sum.at[h, i], far_in.at[h], send_f.at[h], recv_f.at[h])
    wait_all(again)
    slab_in[2, at.z] = slabs[1]
    for i in range(RING):
        top_ref[0, pl.ds(i * DEPTH, DEPTH)] = slab_in[2, i]
    for h in range(2):
        for up in range(2):
            for t in range(1, SIZE + 1 - up):
                for u in range(PIECES):
                    chain_copy(h, up, t, u).wait_send()
    wait_all(far)
    for h in range(2):
        other, _ = lines[1 - h]
        total = near_sum[h, other].astype(f32)
        for o in range(1, RING):
            total = total + far_in[h, (other + o) % RING].astype(f32)
        parent_ref[0, pl.ds(h * HALF, HALF)] = total


def per_device(self_blocks, near_blocks, leaf_basis, transfer, near_list, adm_list, parent_kernel, chain_coupling):
    leaves, width = leaf_basis.shape[:2]
    entries = transfer.shape[1]
    order = jnp.arange(leaves * entries, dtype=jnp.int32).reshape(leaves, entries, 1)
    names = adm_list[:, :, None] == jnp.arange(RING * RING, dtype=jnp.int32)[None, None, :]
    inverse = jnp.min(jnp.where(names, order, leaves * entries), axis=1)
    sems = pltpu.SemaphoreType.DMA
    panel = jax.ShapeDtypeStruct((1, RANK, RANK), f32)
    return pl.pallas_call(
        kernel_body,
        out_shape=(jax.ShapeDtypeStruct((leaves, RANK, RANK), f32), panel, panel),
        in_specs=[SMEM] * 3 + [ANY] * 6,
        out_specs=(VMEM, VMEM, VMEM),
        scratch_shapes=[
            pltpu.VMEM((leaves, width, width), bf16),
            pltpu.VMEM((leaves, 1, width, width), bf16),
            pltpu.VMEM((leaves, width, width), bf16),
            pltpu.VMEM((leaves, entries, RANK, RANK), bf16),
            pltpu.VMEM((RING, RING, HALF, RANK), bf16),
            pltpu.VMEM((RING, RING, HALF, RANK), bf16),
            pltpu.VMEM((2 * leaves, width, RANK), bf16),
            pltpu.VMEM((RING, RANK, RANK), f32),
            pltpu.VMEM((leaves, width, width), f32),
            pltpu.VMEM((leaves, RANK, RANK), f32),
            pltpu.VMEM((leaves * entries, RANK, RANK), bf16),
            pltpu.VMEM((leaves * entries + 1, RANK, RANK), bf16),
            pltpu.VMEM((2, RING, RING, HALF, RANK), bf16),
            pltpu.VMEM((2, SIZE, RING, HALF, RANK), bf16),
            pltpu.VMEM((2, SIZE - 1, RING, HALF, RANK), bf16),
            pltpu.VMEM((2, RING, HALF, RANK), bf16),
            pltpu.VMEM((2, RING, HALF, RANK), bf16),
            pltpu.VMEM((RANK, RANK), f32),
            pltpu.VMEM((RING, RANK, RANK), bf16),
            pltpu.VMEM((2, RING * RANK, RANK), bf16),
            pltpu.VMEM((RANK, RANK), f32),
            pltpu.VMEM((2, DEPTH, RANK), f32),
            pltpu.VMEM((3, RING, DEPTH, RANK), f32),
            sems((2 * leaves + 5,)),
            sems((3, RING)), sems((3, RING)),
            sems((2, 2, SIZE + 1)), sems((2, 2, SIZE + 1)),
            sems((2, 2, SIZE + 1, PIECES)), sems((2, 2, SIZE + 1, PIECES)),
            sems((2, RING)), sems((2, RING)),
            sems((RING,)), sems((RING,)),
            sems((3, RING)), sems((3, RING)),
        ],
        compiler_params=pltpu.CompilerParams(
            collective_id=0, has_side_effects=True, vmem_limit_bytes=48 * 2**20
        ),
    )(near_list, adm_list, inverse, self_blocks, near_blocks, leaf_basis, transfer, parent_kernel, chain_coupling)


def solution(mesh):
    lead = P(("grp", "leaf"))
    return jax.shard_map(
        per_device,
        mesh=mesh,
        in_specs=(lead, lead, lead, lead, lead, lead, lead, P("grp")),
        out_specs=(lead, lead, P("grp")),
        check_vma=False,
    )
```

time: 561 us -> 84.3 us (0.15)
  the two profiles are of different devices: /device:TPU:1 before, /device:TPU:56 now
where the time goes in v2:
time: 84.3 us; the launch traced here: 82.8 us
  Pallas kernels  72.3 us (86%)
  local copies, waits for them, and re-layouts  9.82 us (12%)
    pallas_call x1, Pallas kernels, per_device(): pl.pallas_call(kernel_body, out_shape=(jax.ShapeDtypeStruct((leaves, RANK...  72.3 us
    unnamed x18, local copies, waits for them, and re-layouts  9.82 us

profile of v2, /device:TPU:56, one launch (start us, length us, event | category | flops | bytes accessed | tf_op | source)
XLA Modules:
  0.0 82.8 jit_solution(3385542876170451383)
XLA Ops:
  0.6 0.7 copy.12.near_list
  1.4 0.0 copy-start.6
  1.4 0.7 copy-done.6
  2.1 0.1 select_reduce_fusion.inverse
  2.1 0.0 copy-start
  2.2 1.2 %copy-done = bf16[2,512,512]{2,1,0:T(8,128)(2,1)S(1)} copy-done((bf16[2,512,512]{2,1,0:T(8,128)(2,1)S(1)}, bf16[2,512,512]{2,1,0:T(8,128)(2,1)}, u32[]{:S(2)}) %copy-start) | copy-done | bytes 1048600
  3.4 0.0 copy-start.1
  3.4 1.2 %copy-done.1 = bf16[2,1,512,512]{3,2,1,0:T(8,128)(2,1)S(1)} copy-done((bf16[2,1,512,512]{3,2,1,0:T(8,128)(2,1)S(1)}, bf16[2,1,512,512]{3,2,1,0:T(8,128)(2,1)}, u32[]{:S(2)}) %copy-start.1) | copy-done | bytes 1048600
  4.6 0.0 copy-start.2
  4.6 1.2 %copy-done.2 = bf16[2,512,512]{2,1,0:T(8,128)(2,1)S(1)} copy-done((bf16[2,512,512]{2,1,0:T(8,128)(2,1)S(1)}, bf16[2,512,512]{2,1,0:T(8,128)(2,1)}, u32[]{:S(2)}) %copy-start.2) | copy-done | bytes 1048600
  5.8 0.0 copy-start.3
  5.8 1.2 %copy-done.3 = bf16[2,16,128,128]{3,2,1,0:T(8,128)(2,1)S(1)} copy-done((bf16[2,16,128,128]{3,2,1,0:T(8,128)(2,1)S(1)}, bf16[2,16,128,128]{3,2,1,0:T(8,128)(2,1)}, u32[]{:S(2)}) %copy-start.3) | copy-done | bytes 1048600
  7.0 0.0 copy-start.4
  7.0 0.8 %copy-done.4 = f32[1,128,128]{2,1,0:T(8,128)S(1)} copy-done((f32[1,128,128]{2,1,0:T(8,128)S(1)}, f32[1,128,128]{2,1,0:T(8,128)}, u32[]{:S(2)}) %copy-start.4) | copy-done | bytes 65560
  7.9 0.0 copy-start.5
  7.9 0.8 copy-done.5
  8.6 72.3 %shard_map.103 = (f32[2,128,128]{2,1,0:T(8,128)S(1)}, f32[1,128,128]{2,1,0:T(8,128)S(1)}, f32[1,128,128]{2,1,0:T(8,128)S(1)}) custom-call(s32[2,1]{1,0:T(2,128)S(1)} %copy.12.near_list, s32[2,16]{1,0:T(2,128)S(1)} %copy-done.6, s32[2,64]{1,0:T(2,128)S(1)} %select_reduce_fusion.inverse, bf16[2,512,512]{2,1,0:T(8,128)(2,1)S(1)} %copy-done, ...), custom_call_target="tpu_custom_call" | custom-call | tf_op jit(solution)/shard_map/pallas_call | solution.py:458
  80.9 0.7 copy.16
  81.6 0.6 copy.17
  82.2 0.6 copy.18
  (1 shorter events, 0.0 us)
Async XLA Ops:
  1.4 0.7 copy-start.6
  2.1 1.2 %copy-start = (bf16[2,512,512]{2,1,0:T(8,128)(2,1)S(1)}, bf16[2,512,512]{2,1,0:T(8,128)(2,1)}, u32[]{:S(2)}) copy-start(bf16[2,512,512]{2,1,0:T(8,128)(2,1)} %blocks_hbm.1) | copy-start | bytes 3145732
  3.4 1.2 %copy-start.1 = (bf16[2,1,512,512]{3,2,1,0:T(8,128)(2,1)S(1)}, bf16[2,1,512,512]{3,2,1,0:T(8,128)(2,1)}, u32[]{:S(2)}) copy-start(bf16[2,1,512,512]{3,2,1,0:T(8,128)(2,1)} %near_hbm.1) | copy-start | bytes 3145732
  4.6 1.2 %copy-start.2 = (bf16[2,512,512]{2,1,0:T(8,128)(2,1)S(1)}, bf16[2,512,512]{2,1,0:T(8,128)(2,1)}, u32[]{:S(2)}) copy-start(bf16[2,512,512]{2,1,0:T(8,128)(2,1)} %basis_hbm.1) | copy-start | bytes 3145732
  5.8 1.2 %copy-start.3 = (bf16[2,16,128,128]{3,2,1,0:T(8,128)(2,1)S(1)}, bf16[2,16,128,128]{3,2,1,0:T(8,128)(2,1)}, u32[]{:S(2)}) copy-start(bf16[2,16,128,128]{3,2,1,0:T(8,128)(2,1)} %transfer_hbm.1) | copy-start | bytes 3145732
  7.0 0.8 %copy-start.4 = (f32[1,128,128]{2,1,0:T(8,128)S(1)}, f32[1,128,128]{2,1,0:T(8,128)}, u32[]{:S(2)}) copy-start(f32[1,128,128]{2,1,0:T(8,128)} %chain_hbm.1) | copy-start | bytes 196612
  7.9 0.8 copy-start.5

commit v3 on v2

--- a/solution.py
+++ b/solution.py
@@ -13,6 +13,7 @@
 VMEM = pl.BlockSpec(memory_space=pltpu.VMEM)
 SMEM = pl.BlockSpec(memory_space=pltpu.SMEM)
 ANY = pl.BlockSpec(memory_space=pl.ANY)
+HBM = pl.BlockSpec(memory_space=pltpu.HBM)
 RING = 8
 RANK = 128
 HALF = 64
@@ -37,64 +38,90 @@
     )
 
 
-def factor_strip(strip, below, c0):
-    shape = strip.shape
-    lane = lax.broadcasted_iota(jnp.int32, shape, 2)
-    sub = lax.broadcasted_iota(jnp.int32, shape, 1)
-    inside = (lane >= c0) & (lane < c0 + 8)
-    column = lambda x, i: jnp.broadcast_to(x[:, :, c0 + i : c0 + i + 1], shape)
-    row = lambda x, j: jnp.broadcast_to(x[:, j : j + 1], shape)
-    columns = [column(strip, i) for i in range(8)]
-    block = [jnp.stack([row(columns[i], j) for j in range(i, 8)], axis=0) for i in range(8)]
-    rows = jnp.stack(
-        [jnp.where(inside, jnp.where(lane == c0 + j, 1.0, 0.0), row(strip, j)) for j in range(8)], axis=0
-    )
-    following = None
-    if below is not None:
-        left = jnp.stack([column(below, i) for i in range(8)], axis=0)
-        following = jnp.where(inside, 0.0, below)
-    mult, scaled = [], []
-    for k in range(8):
-        pivot = 1.0 / block[k][0]
-        for i in range(k + 1, 8):
-            block[i] = block[i] - (block[k][i - k :] * block[k][i - k]) * pivot
-        scaled.append(rows[0] * pivot)
-        if below is not None:
-            following = following - left[0] * scaled[k]
-        if k < 7:
-            mult.append(block[k][1:] * pivot)
-            rows = rows[1:] - mult[k] * rows[0]
-            if below is not None:
-                left = left[1:] - mult[k] * left[0]
-    rows = jnp.stack(scaled, axis=0)
-    result = None
-    for k in range(7, -1, -1):
-        result = rows[k] if result is None else jnp.where(sub == k, rows[k], result)
-        if k > 0:
-            rows = rows[:k] - jnp.stack([mult[j][k - j - 1] for j in range(k)], axis=0) * rows[k]
-    return result, following
-
-
-def invert(mats, between):
-    leaves = mats.shape[0]
-    lane = lax.broadcasted_iota(jnp.int32, (RANK, RANK), 1)
+def split(x):
+    high = x.astype(bf16)
+    return high, (x - high.astype(f32)).astype(bf16)
+
+
+def dot_split(a, b):
+    (ah, al), (bh, bl) = split(a), split(b)
+    return dot(ah, bh) + (dot(ah, bl) + dot(al, bh))
+
+
+def invert(first, second, between):
+    sub = lax.broadcasted_iota(jnp.int32, TILE, 0)
+    lane = lax.broadcasted_iota(jnp.int32, TILE, 1)
+    lane_all = lax.broadcasted_iota(jnp.int32, (RANK, RANK), 1)
+    upper_half = sub < 4
+    turn = lambda x: pltpu.roll(x, 4, axis=0)
+    pack = lambda x, y: (jnp.where(upper_half, x, turn(y)), jnp.where(upper_half, turn(x), y))
+    spread = lambda x, j: jnp.take_along_axis(x, jnp.where(upper_half, j, 4 + j), axis=0)
     steps = RANK // 8
-    ahead = mats[:, 0:8]
+    strip = pack(first[0:8], second[0:8])
     for s in range(steps):
         c0 = 8 * s
-        strip, ahead = factor_strip(ahead, mats[:, c0 + 8 : c0 + 16] if s + 1 < steps else None, c0)
+        last = s + 1 == steps
         inside = (lane >= c0) & (lane < c0 + 8)
+        column = lambda x, i: jnp.broadcast_to(x[:, c0 + i : c0 + i + 1], TILE)
+        columns = [[column(x, i) for i in range(8)] for x in strip]
+        block = {(j, i): spread(columns[j // 4][i], j % 4) for i in range(8) for j in range(i, 8)}
+        rows = [
+            jnp.where(inside, jnp.where(lane == c0 + j, 1.0, 0.0), spread(strip[j // 4], j % 4)) for j in range(8)
+        ]
+        if not last:
+            below = pack(first[c0 + 8 : c0 + 16], second[c0 + 8 : c0 + 16])
+            left = [[column(x, i) for i in range(8)] for x in below]
+            following = [jnp.where(inside, 0.0, x) for x in below]
+        mult = {}
+        for k in range(8):
+            pivot = 1.0 / block[k, k]
+            for j in range(k + 1, 8):
+                mult[j, k] = block[j, k] * pivot
+            for j in range(k + 1, 8):
+                for i in range(k + 1, j + 1):
+                    block[j, i] = block[j, i] - mult[j, k] * block[i, k]
+                rows[j] = rows[j] - mult[j, k] * rows[k]
+            rows[k] = rows[k] * pivot
+            if not last:
+                for q in range(2):
+                    following[q] = following[q] - left[q][k] * rows[k]
+                    for j in range(k + 1, 8):
+                        left[q][j] = left[q][j] - mult[j, k] * left[q][k]
+        for k in range(7, 0, -1):
+            for j in range(k):
+                rows[j] = rows[j] - mult[k, j] * rows[k]
+        kept, turned = rows[0], rows[4]
+        for j in range(1, 8):
+            kept = jnp.where(sub == j, rows[j], kept)
+            turned = jnp.where(sub == j, rows[(j + 4) % 8], turned)
+        turned = turn(turned)
+        inside_all = (lane_all >= c0) & (lane_all < c0 + 8)
+        nothing = jnp.zeros(TILE, f32)
         results = []
-        for l in range(leaves):
-            nothing = jnp.zeros(TILE, f32)
-            placed = jnp.concatenate([strip[l] if t == s else nothing for t in range(steps)], axis=0)
-            rest = jnp.where(inside, 0.0, mats[l]) - dot_full(mats[l], placed)
+        for a, done in (
+            (first, jnp.where(upper_half, kept, turned)),
+            (second, jnp.where(upper_half, turned, kept)),
+        ):
+            high = done.astype(bf16).astype(f32)
+            place = lambda x: jnp.concatenate([x if t == s else nothing for t in range(steps)], axis=0).astype(bf16)
+            zh, zl = place(high), place(done - high)
+            wide = jnp.concatenate(
+                [
+                    jnp.concatenate([zh, zl], axis=1),
+                    jnp.concatenate([zh, jnp.zeros((RANK, RANK), bf16)], axis=1),
+                ],
+                axis=0,
+            )
+            product = dot(jnp.concatenate(split(a), axis=1), wide)
+            rest = jnp.where(inside_all, 0.0, a) - (product[:, :RANK] + product[:, RANK:])
             results.append(
-                jnp.concatenate([strip[l] if t == s else rest[8 * t : 8 * t + 8] for t in range(steps)], axis=0)
+                jnp.concatenate([done if t == s else rest[8 * t : 8 * t + 8] for t in range(steps)], axis=0)
             )
-        mats = jnp.stack(results, axis=0)
+        first, second = results
+        if not last:
+            strip = following
         between(s)
-    return mats
+    return first, second
 
 
 def form_reduced(l, parts, blocks, basis, reduced):
@@ -113,7 +140,7 @@
     @pl.loop(0, parts - 1)
     def _(k):
         here = pl.ds(pl.multiple_of(k * RANK, RANK), RANK)
-        inverses[...] = invert(reduced[:, here, here], functools.partial(between, k))
+        inverses[0], inverses[1] = invert(reduced[0, here, here], reduced[1, here, here], functools.partial(between, k))
         for known in range(parts - 1):
 
             @pl.when(k == known)
@@ -121,8 +148,8 @@
                 here = pl.ds(RANK * known, RANK)
                 rest = pl.ds(RANK * (known + 1), RANK * (parts - 1 - known))
                 for l in range(leaves):
-                    solved = dot_full(inverses[l], reduced[l, here, rest])
-                    reduced[l, rest, rest] = reduced[l, rest, rest] - dot_full(reduced[l, rest, here], solved)
+                    solved = dot_split(inverses[l], reduced[l, here, rest])
+                    reduced[l, rest, rest] = reduced[l, rest, rest] - dot_split(reduced[l, rest, here], solved)
 
 
 class Places:
@@ -188,11 +215,15 @@
 SIZE = RING // 2
 PIECES = 2
 DEPTH = RANK // RING
-GATHER_AT = {(0, 3): 1, (0, 15): 2, (1, 13): 3, (2, 9): 4}
+SPAN = RING // PIECES
+GATHER_AT = [
+    ((0, 3), 1, 0), ((0, 3), 1, 1), ((1, 0), 2, 0), ((1, 2), 2, 1),
+    ((1, 14), 3, 0), ((2, 0), 3, 1), ((2, 10), 4, 0), ((2, 13), 4, 1),
+]
 
 
 def kernel_body(
-    near_list, adm, inverse, blocks_hbm, near_hbm, basis_hbm, transfer_hbm, kernel_hbm, chain_hbm,
+    table, blocks_hbm, near_hbm, basis_hbm, transfer_hbm, kernel_hbm, chain_hbm,
     panels_ref, parent_ref, top_ref,
     blocks, near, basis, transfer, upper, lower, halo, maps, reduced, inverses, lifted, terms, shares,
     down_in, up_in, near_sum, far_in, local, local_in, prefix, cross, slabs, slab_in,
@@ -213,35 +244,30 @@
     loads += [(near_hbm, near), (transfer_hbm, transfer)]
     loads += [(top, upper.at[at.y, at.z]), (bottom, lower.at[at.z, at.y]), (chain_hbm.at[0], maps.at[at.grp])]
     loads = [pltpu.make_async_copy(src, dst, load_sem.at[i]) for i, (src, dst) in enumerate(loads)]
+    greet(at)
     for load in loads:
         load.start()
-    greet(at)
+    await_greetings(at)
+    exchange(at.z, at.on_z, lambda i: top, upper.at[at.y], send_1.at[0], recv_1.at[0])
+    exchange(at.y, at.on_y, lambda i: bottom, lower.at[at.z], send_1.at[1], recv_1.at[1])
+    exchange(at.grp, at.on_grp, lambda i: chain_hbm.at[0], maps, send_1.at[2], recv_1.at[2])
 
     for l in range(leaves):
         loads[2 * l].wait()
         loads[2 * l + 1].wait()
         form_reduced(l, parts, blocks, basis, reduced)
-        if l == 0:
-            await_greetings(at)
-            exchange(at.z, at.on_z, lambda i: top, upper.at[at.y], send_1.at[0], recv_1.at[0])
-            exchange(at.y, at.on_y, lambda i: bottom, lower.at[at.z], send_1.at[1], recv_1.at[1])
-            exchange(at.grp, at.on_grp, lambda i: chain_hbm.at[0], maps, send_1.at[2], recv_1.at[2])
-
-    def gather_copies(t):
+
+    def gather_copies(t, u):
         copies = []
+        piece = pl.ds(u * SPAN, SPAN)
         for h, (table, pos, to) in enumerate(((upper, at.y, at.on_y), (lower, at.z, at.on_z))):
-            chunk = (pos - t + 1 + RING) % RING
-            copies.append(
-                remote(table.at[chunk], table.at[chunk], send_2.at[h, 0, t], recv_2.at[h, 0, t], to((pos + 1) % RING))
-            )
-            if t < SIZE:
-                chunk = (pos + t - 1) % RING
-                copies.append(
-                    remote(
-                        table.at[chunk], table.at[chunk], send_2.at[h, 1, t], recv_2.at[h, 1, t],
-                        to((pos + RING - 1) % RING),
-                    )
-                )
+            for up in range(2):
+                if t == SIZE and not up:
+                    continue
+                chunk = (pos - t + 1 + RING) % RING if up else (pos + t - 1) % RING
+                target = (pos + 1) % RING if up else (pos + RING - 1) % RING
+                part = table.at[chunk, piece]
+                copies.append(remote(part, part, send_2.at[h, up, t, u], recv_2.at[h, up, t, u], to(target)))
         return copies
 
     def halo_copies():
@@ -261,20 +287,21 @@
         ]
 
     def between(k, s):
-        for (block, step), t in GATHER_AT.items():
+        for (block, step), t, u in GATHER_AT:
             if s == step:
 
                 @pl.when(k == block)
-                def _(t=t):
-                    if t == 1:
+                def _(t=t, u=u):
+                    if t > 1:
+                        for copy in gather_copies(t - 1, u):
+                            copy.wait_recv()
+                    elif u == 0:
                         loads[-3].wait()
                         loads[-2].wait()
                         wait_all(first_copies())
-                    else:
-                        wait_all(gather_copies(t - 1))
-                    for copy in gather_copies(t):
+                    for copy in gather_copies(t, u):
                         copy.start()
-                    if t == SIZE:
+                    if t == SIZE and u == PIECES - 1:
                         for copy in halo_copies():
                             copy.start()
 
@@ -291,7 +318,9 @@
                 a = step * group + i
                 lifted[l * entries + a] = dot(lowered, transfer[l, a]).astype(bf16)
 
-    wait_all(gather_copies(SIZE))
+    for u in range(PIECES):
+        for copy in gather_copies(SIZE, u):
+            copy.wait_recv()
     local[...] = jnp.zeros_like(local)
 
     for l in range(leaves):
@@ -301,7 +330,7 @@
             total = None
             for i in range(group):
                 a = step * group + i
-                p = adm[l, a]
+                p = table[l, RING * RING + a]
                 pz, py = p // RING, p % RING
                 panel = lifted[l * entries + a]
                 kernel = jnp.concatenate([upper[py, pz], lower[pz, py]], axis=0)
@@ -319,18 +348,16 @@
     def _(pz):
         for py in range(RING):
             p = pz * RING + py
-            share = terms[inverse[0, p]].astype(f32)
+            share = terms[table[0, p]].astype(f32)
             for l in range(1, leaves):
-                share = share + terms[inverse[l, p]].astype(f32)
+                share = share + terms[table[l, p]].astype(f32)
             share = share.astype(bf16)
             shares[0, pz, py] = share[:HALF]
             shares[1, py, pz] = share[HALF:]
 
-    span = RING // PIECES
-
     def chain_copy(h, up, t, u):
         pos, to = lines[h]
-        piece = pl.ds(u * span, span)
+        piece = pl.ds(u * SPAN, SPAN)
         buffer = (down_in, up_in)[up]
         chunk = (pos + 4 - t + RING) % RING if up else (pos - 5 + t + RING) % RING
         src = shares.at[h, chunk, piece] if t == 1 else buffer.at[h, t - 2, piece]
@@ -347,7 +374,7 @@
                     if up and t == SIZE:
                         continue
                     if t > 1:
-                        piece = pl.ds(u * span, span)
+                        piece = pl.ds(u * SPAN, SPAN)
                         buffer = (down_in, up_in)[up]
                         chunk = (pos + 4 - t + RING) % RING if up else (pos - 5 + t + RING) % RING
                         mine = shares[h, chunk, piece].astype(f32)
@@ -400,35 +427,50 @@
 
     by_z = exchange(at.z, at.on_z, lambda i: cross.at[slab(i)], slab_in.at[0], send_r.at[0], recv_r.at[0])
 
+    chain_step(3)
+
     for copy in halo_copies():
         copy.wait()
     loads[2 * leaves].wait()
     first = ((at.grp * lax.axis_size("leaf") + at.leaf) - 1) * leaves
     for l in range(leaves):
-        place = near_list[l, 0] - first
+        place = table[l, RING * RING + entries] - first
         place = jnp.clip(jnp.where(place < leaves, place, place - leaves), 0, 2 * leaves - 1)
         facing = dot_t(basis[l, :, skeleton], near[l, 0]).astype(bf16)
         panels_ref[l] = reduced[l, skeleton, skeleton] + dot(facing, halo[place])
 
-    chain_step(3)
+    chain_step(4)
     wait_all(by_z)
     slabs[0] = gathered(0, at.z, cross[slab(at.z)])
     by_y = exchange(at.y, at.on_y, lambda i: slabs.at[0], slab_in.at[1], send_r.at[1], recv_r.at[1])
-    chain_step(4)
+
+    def far_copy(h, i):
+        other, to = lines[1 - h]
+        return remote(near_sum.at[h, i], far_in.at[h, other], send_f.at[h, i], recv_f.at[h, other], to(i))
+
+    for u in range(PIECES):
+        piece = pl.ds(u * SPAN, SPAN)
+        for h in range(2):
+            pos, _ = lines[h]
+            chain_copy(h, 0, SIZE, u).wait_recv()
+            near_sum[h, piece] = (
+                down_in[h, SIZE - 1, piece].astype(f32)
+                + up_in[h, SIZE - 2, piece].astype(f32)
+                + shares[h, pos, piece].astype(f32)
+            ).astype(bf16)
+            for i in range(u * SPAN, (u + 1) * SPAN):
+
+                @pl.when(i != lines[1 - h][0])
+                def _(h=h, i=i):
+                    far_copy(h, i).start()
+
     wait_all(by_y)
     slabs[1] = gathered(1, at.y, slabs[0])
     again = exchange(at.z, at.on_z, lambda i: slabs.at[1], slab_in.at[2], send_r.at[2], recv_r.at[2])
-
-    far = []
-    for h in range(2):
-        pos, _ = lines[h]
+    for t in range(1, SIZE + 1):
         for u in range(PIECES):
-            chain_copy(h, 0, SIZE, u).wait_recv()
-        near_sum[h] = (
-            down_in[h, SIZE - 1].astype(f32) + up_in[h, SIZE - 2].astype(f32) + shares[h, pos].astype(f32)
-        ).astype(bf16)
-        other, to = lines[1 - h]
-        far += exchange(other, to, lambda i, h=h: near_sum.at[h, i], far_in.at[h], send_f.at[h], recv_f.at[h])
+            for copy in gather_copies(t, u):
+                copy.wait_send()
     wait_all(again)
     slab_in[2, at.z] = slabs[1]
     for i in range(RING):
@@ -438,13 +480,20 @@
             for t in range(1, SIZE + 1 - up):
                 for u in range(PIECES):
                     chain_copy(h, up, t, u).wait_send()
-    wait_all(far)
     for h in range(2):
-        other, _ = lines[1 - h]
+        other, to = lines[1 - h]
         total = near_sum[h, other].astype(f32)
         for o in range(1, RING):
-            total = total + far_in[h, (other + o) % RING].astype(f32)
+            i = (other + o) % RING
+            far_copy(h, i).wait_send()
+            remote(near_sum.at[h, i], far_in.at[h, i], send_f.at[h, i], recv_f.at[h, i], to(i)).wait_recv()
+            total = total + far_in[h, i].astype(f32)
         parent_ref[0, pl.ds(h * HALF, HALF)] = total
+
+
+def hand_out(*refs):
+    for i in range(3):
+        refs[3 + i][...] = refs[i][...]
 
 
 def per_device(self_blocks, near_blocks, leaf_basis, transfer, near_list, adm_list, parent_kernel, chain_coupling):
@@ -453,12 +502,13 @@
     order = jnp.arange(leaves * entries, dtype=jnp.int32).reshape(leaves, entries, 1)
     names = adm_list[:, :, None] == jnp.arange(RING * RING, dtype=jnp.int32)[None, None, :]
     inverse = jnp.min(jnp.where(names, order, leaves * entries), axis=1)
+    table = jnp.concatenate([inverse, adm_list, near_list], axis=1)
     sems = pltpu.SemaphoreType.DMA
     panel = jax.ShapeDtypeStruct((1, RANK, RANK), f32)
-    return pl.pallas_call(
+    results = pl.pallas_call(
         kernel_body,
         out_shape=(jax.ShapeDtypeStruct((leaves, RANK, RANK), f32), panel, panel),
-        in_specs=[SMEM] * 3 + [ANY] * 6,
+        in_specs=[SMEM] + [HBM] * 6,
         out_specs=(VMEM, VMEM, VMEM),
         scratch_shapes=[
             pltpu.VMEM((leaves, width, width), bf16),
@@ -486,16 +536,23 @@
             pltpu.VMEM((3, RING, DEPTH, RANK), f32),
             sems((2 * leaves + 5,)),
             sems((3, RING)), sems((3, RING)),
-            sems((2, 2, SIZE + 1)), sems((2, 2, SIZE + 1)),
+            sems((2, 2, SIZE + 1, PIECES)), sems((2, 2, SIZE + 1, PIECES)),
             sems((2, 2, SIZE + 1, PIECES)), sems((2, 2, SIZE + 1, PIECES)),
             sems((2, RING)), sems((2, RING)),
             sems((RING,)), sems((RING,)),
             sems((3, RING)), sems((3, RING)),
         ],
         compiler_params=pltpu.CompilerParams(
-            collective_id=0, has_side_effects=True, vmem_limit_bytes=48 * 2**20
+            collective_id=0, has_side_effects=True, vmem_limit_bytes=58 * 2**20
         ),
-    )(near_list, adm_list, inverse, self_blocks, near_blocks, leaf_basis, transfer, parent_kernel, chain_coupling)
+    )(table, self_blocks, near_blocks, leaf_basis, transfer, parent_kernel, chain_coupling)
+    return pl.pallas_call(
+        hand_out,
+        out_shape=tuple(jax.ShapeDtypeStruct(r.shape, r.dtype) for r in results),
+        in_specs=[VMEM] * 3,
+        out_specs=(VMEM,) * 3,
+        compiler_params=pltpu.CompilerParams(vmem_limit_bytes=58 * 2**20),
+    )(*results)
 
 
 def solution(mesh):

time: 84.3 us -> 76.2 us (0.904)
  local copies, waits for them, and re-layouts: 9.82 us -> 1.41 us
    unnamed x18 -> x3, local copies, waits for them, and re-layouts: 9.82 us -> 1.41 us
    pallas_call x1, Pallas kernels: 72.3 us -> 70.5 us  [per_device(): pl.pallas_call(kernel_body, out_shape=(jax.ShapeDtypeStruct((leaves, RANK...]
    pallas_call x0 -> x1, Pallas kernels: none -> 1.65 us  [per_device(): pl.pallas_call(hand_out, out_shape=tuple((jax.ShapeDtypeStruct(r.shape, r...]
where the time goes in v3:
time: 76.2 us; the launch traced here: 74.9 us
  Pallas kernels  72.1 us (95%)
  local copies, waits for them, and re-layouts  1.41 us (2%)
    pallas_call x1, Pallas kernels, per_device(): pl.pallas_call(kernel_body, out_shape=(jax.ShapeDtypeStruct((leaves, RANK...  70.5 us
    pallas_call x1, Pallas kernels, per_device(): pl.pallas_call(hand_out, out_shape=tuple((jax.ShapeDtypeStruct(r.shape, r...  1.65 us

profile of v3, /device:TPU:56, one launch (start us, length us, event | category | flops | bytes accessed | tf_op | source)
XLA Modules:
  0.0 74.9 jit_solution(3129102232194452980)
XLA Ops:
  0.6 0.7 copy.12
  1.4 0.0 copy-start
  1.4 0.7 copy-done
  2.1 0.1 select_reduce_fusion
  2.1 0.6 pad_add_fusion.table
  2.8 70.5 %shard_map.103 = (f32[2,128,128]{2,1,0:T(8,128)}, f32[1,128,128]{2,1,0:T(8,128)}, f32[1,128,128]{2,1,0:T(8,128)}) custom-call(s32[2,81]{1,0:T(2,128)} %pad_add_fusion.table, bf16[2,512,512]{2,1,0:T(8,128)(2,1)} %blocks_hbm.1, bf16[2,1,512,512]{3,2,1,0:T(8,128)(2,1)} %near_hbm.1, bf16[2,512,512]{2,1,0:T(8,128)(2,1)} %basis_hbm.1, ...), custom_call_target="tpu_custom_call" | custom-call | tf_op jit(solution)/shard_map/pallas_call | solution.py:508
  73.3 1.6 %shard_map.104 = (f32[2,128,128]{2,1,0:T(8,128)}, f32[1,128,128]{2,1,0:T(8,128)}, f32[1,128,128]{2,1,0:T(8,128)}) custom-call(f32[2,128,128]{2,1,0:T(8,128)} %get-tuple-element.6.refs_0_, f32[1,128,128]{2,1,0:T(8,128)} %get-tuple-element.7.refs_1_, f32[1,128,128]{2,1,0:T(8,128)} %get-tuple-element.8.refs_2_), custom_call_target="tpu_custom_call" | custom-call | tf_op jit(solution)/shard_map/pallas_call | solution.py:549
  (1 shorter events, 0.0 us)
Async XLA Ops:
  1.4 0.7 copy-start

commit v4 on v3

--- a/solution.py
+++ b/solution.py
@@ -217,17 +217,16 @@
 DEPTH = RANK // RING
 SPAN = RING // PIECES
 GATHER_AT = [
-    ((0, 3), 1, 0), ((0, 3), 1, 1), ((1, 0), 2, 0), ((1, 2), 2, 1),
-    ((1, 14), 3, 0), ((2, 0), 3, 1), ((2, 10), 4, 0), ((2, 13), 4, 1),
+    ((0, 14), 2, 0), ((0, 15), 2, 1), ((1, 11), 3, 0), ((1, 13), 3, 1), ((2, 11), 4, 0), ((2, 13), 4, 1),
 ]
 
 
 def kernel_body(
-    table, blocks_hbm, near_hbm, basis_hbm, transfer_hbm, kernel_hbm, chain_hbm,
-    panels_ref, parent_ref, top_ref,
+    adm, near_list, blocks_hbm, near_hbm, basis_hbm, transfer_hbm, kernel_hbm, chain_hbm,
+    panels_hbm, parent_hbm, top_hbm,
     blocks, near, basis, transfer, upper, lower, halo, maps, reduced, inverses, lifted, terms, shares,
-    down_in, up_in, near_sum, far_in, local, local_in, prefix, cross, slabs, slab_in,
-    load_sem, send_1, recv_1, send_2, recv_2, send_c, recv_c, send_f, recv_f, send_g, recv_g, send_r, recv_r,
+    down_in, up_in, near_sum, far_in, facing, local_in, prefix, prefix_t, cross, slabs, slab_in, inverse, where, panels_ref, parent_ref, top_ref,
+    load_sem, send_1, recv_1, send_2, recv_2, send_c, recv_c, send_f, recv_f, send_g, recv_g, send_r, recv_r, out_sem,
 ):
     at = Places()
     leaves, width = basis.shape[:2]
@@ -244,13 +243,26 @@
     loads += [(near_hbm, near), (transfer_hbm, transfer)]
     loads += [(top, upper.at[at.y, at.z]), (bottom, lower.at[at.z, at.y]), (chain_hbm.at[0], maps.at[at.grp])]
     loads = [pltpu.make_async_copy(src, dst, load_sem.at[i]) for i, (src, dst) in enumerate(loads)]
+    results = ((panels_ref, panels_hbm), (parent_ref, parent_hbm), (top_ref, top_hbm))
+    results = [pltpu.make_async_copy(src, dst, out_sem.at[i]) for i, (src, dst) in enumerate(results)]
     greet(at)
-    for load in loads:
-        load.start()
+    loads[0].start()
+    loads[1].start()
     await_greetings(at)
     exchange(at.z, at.on_z, lambda i: top, upper.at[at.y], send_1.at[0], recv_1.at[0])
     exchange(at.y, at.on_y, lambda i: bottom, lower.at[at.z], send_1.at[1], recv_1.at[1])
-    exchange(at.grp, at.on_grp, lambda i: chain_hbm.at[0], maps, send_1.at[2], recv_1.at[2])
+    for load in loads[2 : 2 * leaves] + loads[-3:-1]:
+        load.start()
+
+    column = lax.broadcasted_iota(jnp.int32, TILE, 1)
+    row = lax.broadcasted_iota(jnp.int32, TILE, 0)
+    places = jnp.full(TILE, leaves * entries, jnp.int32)
+    for l in range(leaves):
+        for a in range(entries):
+            places = jnp.where((column == adm[l, a]) & (row == l), l * entries + a, places)
+    inverse[...] = places
+    to_scalars = pltpu.make_async_copy(inverse, where, load_sem.at[2 * leaves + 5])
+    to_scalars.start()
 
     for l in range(leaves):
         loads[2 * l].wait()
@@ -292,65 +304,103 @@
 
                 @pl.when(k == block)
                 def _(t=t, u=u):
-                    if t > 1:
-                        for copy in gather_copies(t - 1, u):
-                            copy.wait_recv()
-                    elif u == 0:
-                        loads[-3].wait()
-                        loads[-2].wait()
-                        wait_all(first_copies())
+                    for copy in gather_copies(t - 1, u):
+                        copy.wait_recv()
                     for copy in gather_copies(t, u):
                         copy.start()
-                    if t == SIZE and u == PIECES - 1:
-                        for copy in halo_copies():
-                            copy.start()
-
+                    if (t, u) == (2, PIECES - 1):
+                        exchange(at.grp, at.on_grp, lambda i: chain_hbm.at[0], maps, send_1.at[2], recv_1.at[2])
+
+        if s == 4:
+
+            @pl.when(k == 1)
+            def _():
+                loads[2 * leaves].wait()
+                for l in range(leaves):
+                    facing[l] = dot_t(basis[l, :, skeleton], near[l, 0]).astype(bf16)
+
+    loads[-3].wait()
+    loads[-2].wait()
+    wait_all(first_copies())
+    for u in range(PIECES):
+        for copy in gather_copies(1, u):
+            copy.start()
+    for load in (loads[2 * leaves], loads[2 * leaves + 1], loads[-1]):
+        load.start()
     eliminate(leaves, parts, reduced, inverses, between)
 
     loads[2 * leaves + 1].wait()
-    group = 8
     for l in range(leaves):
         lowered = reduced[l, skeleton, skeleton].astype(bf16)
-
-        @pl.loop(0, entries // group)
-        def _(step, l=l, lowered=lowered):
-            for i in range(group):
-                a = step * group + i
-                lifted[l * entries + a] = dot(lowered, transfer[l, a]).astype(bf16)
+        for a in range(0, entries, 2):
+            pair = dot(lowered, jnp.concatenate([transfer[l, a], transfer[l, a + 1]], axis=1)).astype(bf16)
+            lifted[l * entries + a] = pair[:, :RANK]
+            lifted[l * entries + a + 1] = pair[:, RANK:]
+
+    wait_all(
+        [
+            remote(chain_hbm.at[0], maps.at[at.grp], send_1.at[2, o], recv_1.at[2, o], at.on_grp((at.grp + o) % RING))
+            for o in range(1, RING)
+        ]
+    )
+    loads[-1].wait()
+    eye = (
+        lax.broadcasted_iota(jnp.int32, (RANK, RANK), 0) == lax.broadcasted_iota(jnp.int32, (RANK, RANK), 1)
+    ).astype(f32)
+    running = jnp.zeros((RANK, RANK), f32)
+    for j in range(RING - 1, -1, -1):
+        if j < RING - 1:
+            step_map = 0.8 * eye + 0.5 * maps[j + 1]
+            running = jnp.where(j < at.grp, dot_split(step_map, running), 0.0)
+        running = jnp.where(j == at.grp, eye, running)
+        prefix[j] = jnp.concatenate(split(running), axis=0)
+        turned = split(running.T)
+        for q in range(2):
+            prefix_t[q, :, pl.ds(j * RANK, RANK)] = turned[q]
 
     for u in range(PIECES):
         for copy in gather_copies(SIZE, u):
             copy.wait_recv()
-    local[...] = jnp.zeros_like(local)
-
+    for copy in halo_copies():
+        copy.start()
+    nothing = jnp.zeros((RANK, RANK), bf16)
+
+    def diagonal(x, y):
+        return jnp.concatenate(
+            [jnp.concatenate([x, nothing], axis=1), jnp.concatenate([nothing, y], axis=1)], axis=0
+        )
+
+    total = None
     for l in range(leaves):
-
-        @pl.loop(0, entries // group)
-        def _(step, l=l):
-            total = None
-            for i in range(group):
-                a = step * group + i
-                p = table[l, RING * RING + a]
+        for a in range(0, entries, 2):
+            panels = [lifted[l * entries + a + q] for q in range(2)]
+            kernels = []
+            for q in range(2):
+                p = adm[l, a + q]
                 pz, py = p // RING, p % RING
-                panel = lifted[l * entries + a]
-                kernel = jnp.concatenate([upper[py, pz], lower[pz, py]], axis=0)
-                mixture = dot(kernel, panel).astype(bf16)
-                term = dot_t(panel, mixture)
-                terms[l * entries + a] = term.astype(bf16)
-                total = term if total is None else total + term
-            local[...] += total
+                kernels.append(jnp.concatenate([upper[py, pz], lower[pz, py]], axis=0))
+            mixture = dot(jnp.concatenate(kernels, axis=1), diagonal(*panels)).astype(bf16)
+            term = dot(
+                jnp.concatenate([panel.T for panel in panels], axis=1),
+                diagonal(mixture[:, :RANK], mixture[:, RANK:]),
+            )
+            for q in range(2):
+                part = term[:, q * RANK : (q + 1) * RANK]
+                terms[l * entries + a + q] = part.astype(bf16)
+                total = part if total is None else total + part
 
     terms[leaves * entries] = jnp.zeros((RANK, RANK), bf16)
-    local_in[at.grp] = local[...].astype(bf16)
+    to_scalars.wait()
+    local_in[at.grp] = total.astype(bf16)
     by_grp = exchange(at.grp, at.on_grp, lambda i: local_in.at[at.grp], local_in, send_g, recv_g)
 
     @pl.loop(0, RING)
     def _(pz):
         for py in range(RING):
             p = pz * RING + py
-            share = terms[table[0, p]].astype(f32)
+            share = terms[where[0, p]].astype(f32)
             for l in range(1, leaves):
-                share = share + terms[table[l, p]].astype(f32)
+                share = share + terms[where[l, p]].astype(f32)
             share = share.astype(bf16)
             shares[0, pz, py] = share[:HALF]
             shares[1, py, pz] = share[HALF:]
@@ -383,39 +433,15 @@
 
     chain_step(1)
 
-    wait_all(
-        [
-            remote(chain_hbm.at[0], maps.at[at.grp], send_1.at[2, o], recv_1.at[2, o], at.on_grp((at.grp + o) % RING))
-            for o in range(1, RING)
-        ]
-    )
-    loads[-1].wait()
-    eye = (
-        lax.broadcasted_iota(jnp.int32, (RANK, RANK), 0) == lax.broadcasted_iota(jnp.int32, (RANK, RANK), 1)
-    ).astype(f32)
-    running = jnp.zeros((RANK, RANK), f32)
-    for j in range(RING - 1, -1, -1):
-        if j < RING - 1:
-            step_map = 0.8 * eye + 0.5 * maps[j + 1]
-            running = jnp.where(j < at.grp, dot_full(step_map, running), 0.0)
-        running = jnp.where(j == at.grp, eye, running)
-        high = running.astype(bf16)
-        prefix[0, pl.ds(j * RANK, RANK)] = high
-        prefix[1, pl.ds(j * RANK, RANK)] = (running - high.astype(f32)).astype(bf16)
-
     chain_step(2)
 
     wait_all(by_grp)
-    mapped = jnp.concatenate(
-        [
-            dot(local_in[j], prefix[0, pl.ds(j * RANK, RANK)]) + dot(local_in[j], prefix[1, pl.ds(j * RANK, RANK)])
-            for j in range(RING)
-        ],
-        axis=0,
-    )
-    high = mapped.astype(bf16)
-    low = (mapped - high.astype(f32)).astype(bf16)
-    cross[...] = (dot_t(prefix[0], high) + (dot_t(prefix[1], high) + dot_t(prefix[0], low))) * (1.0 / (RING * RING))
+    mapped = []
+    for j in range(RING):
+        root = local_in[j]
+        mapped.append(dot(jnp.concatenate([root, root], axis=1), prefix[j]))
+    high, low = split(jnp.concatenate(mapped, axis=0))
+    cross[...] = (dot(prefix_t[0], high) + (dot(prefix_t[1], high) + dot(prefix_t[0], low))) * (1.0 / (RING * RING))
 
     slab = lambda i: pl.ds(pl.multiple_of(i * DEPTH, DEPTH), DEPTH)
 
@@ -431,18 +457,17 @@
 
     for copy in halo_copies():
         copy.wait()
-    loads[2 * leaves].wait()
     first = ((at.grp * lax.axis_size("leaf") + at.leaf) - 1) * leaves
     for l in range(leaves):
-        place = table[l, RING * RING + entries] - first
+        place = near_list[0, l] - first
         place = jnp.clip(jnp.where(place < leaves, place, place - leaves), 0, 2 * leaves - 1)
-        facing = dot_t(basis[l, :, skeleton], near[l, 0]).astype(bf16)
-        panels_ref[l] = reduced[l, skeleton, skeleton] + dot(facing, halo[place])
-
-    chain_step(4)
+        panels_ref[l] = reduced[l, skeleton, skeleton] + dot(facing[l], halo[place])
+    results[0].start()
+
     wait_all(by_z)
     slabs[0] = gathered(0, at.z, cross[slab(at.z)])
     by_y = exchange(at.y, at.on_y, lambda i: slabs.at[0], slab_in.at[1], send_r.at[1], recv_r.at[1])
+    chain_step(4)
 
     def far_copy(h, i):
         other, to = lines[1 - h]
@@ -475,6 +500,7 @@
     slab_in[2, at.z] = slabs[1]
     for i in range(RING):
         top_ref[0, pl.ds(i * DEPTH, DEPTH)] = slab_in[2, i]
+    results[2].start()
     for h in range(2):
         for up in range(2):
             for t in range(1, SIZE + 1 - up):
@@ -489,6 +515,8 @@
             remote(near_sum.at[h, i], far_in.at[h, i], send_f.at[h, i], recv_f.at[h, i], to(i)).wait_recv()
             total = total + far_in[h, i].astype(f32)
         parent_ref[0, pl.ds(h * HALF, HALF)] = total
+    results[1].start()
+    wait_all(results)
 
 
 def hand_out(*refs):
@@ -499,17 +527,13 @@
 def per_device(self_blocks, near_blocks, leaf_basis, transfer, near_list, adm_list, parent_kernel, chain_coupling):
     leaves, width = leaf_basis.shape[:2]
     entries = transfer.shape[1]
-    order = jnp.arange(leaves * entries, dtype=jnp.int32).reshape(leaves, entries, 1)
-    names = adm_list[:, :, None] == jnp.arange(RING * RING, dtype=jnp.int32)[None, None, :]
-    inverse = jnp.min(jnp.where(names, order, leaves * entries), axis=1)
-    table = jnp.concatenate([inverse, adm_list, near_list], axis=1)
     sems = pltpu.SemaphoreType.DMA
     panel = jax.ShapeDtypeStruct((1, RANK, RANK), f32)
     results = pl.pallas_call(
         kernel_body,
         out_shape=(jax.ShapeDtypeStruct((leaves, RANK, RANK), f32), panel, panel),
-        in_specs=[SMEM] + [HBM] * 6,
-        out_specs=(VMEM, VMEM, VMEM),
+        in_specs=[SMEM] * 2 + [HBM] * 6,
+        out_specs=(HBM,) * 3,
         scratch_shapes=[
             pltpu.VMEM((leaves, width, width), bf16),
             pltpu.VMEM((leaves, 1, width, width), bf16),
@@ -528,24 +552,31 @@
             pltpu.VMEM((2, SIZE - 1, RING, HALF, RANK), bf16),
             pltpu.VMEM((2, RING, HALF, RANK), bf16),
             pltpu.VMEM((2, RING, HALF, RANK), bf16),
-            pltpu.VMEM((RANK, RANK), f32),
+            pltpu.VMEM((leaves, RANK, width), bf16),
             pltpu.VMEM((RING, RANK, RANK), bf16),
-            pltpu.VMEM((2, RING * RANK, RANK), bf16),
+            pltpu.VMEM((RING, 2 * RANK, RANK), bf16),
+            pltpu.VMEM((2, RANK, RING * RANK), bf16),
             pltpu.VMEM((RANK, RANK), f32),
             pltpu.VMEM((2, DEPTH, RANK), f32),
             pltpu.VMEM((3, RING, DEPTH, RANK), f32),
-            sems((2 * leaves + 5,)),
+            pltpu.VMEM(TILE, jnp.int32),
+            pltpu.SMEM(TILE, jnp.int32),
+            pltpu.VMEM((leaves, RANK, RANK), f32),
+            pltpu.VMEM((1, RANK, RANK), f32),
+            pltpu.VMEM((1, RANK, RANK), f32),
+            sems((2 * leaves + 6,)),
             sems((3, RING)), sems((3, RING)),
             sems((2, 2, SIZE + 1, PIECES)), sems((2, 2, SIZE + 1, PIECES)),
             sems((2, 2, SIZE + 1, PIECES)), sems((2, 2, SIZE + 1, PIECES)),
             sems((2, RING)), sems((2, RING)),
             sems((RING,)), sems((RING,)),
             sems((3, RING)), sems((3, RING)),
+            sems((3,)),
         ],
         compiler_params=pltpu.CompilerParams(
             collective_id=0, has_side_effects=True, vmem_limit_bytes=58 * 2**20
         ),
-    )(table, self_blocks, near_blocks, leaf_basis, transfer, parent_kernel, chain_coupling)
+    )(adm_list, near_list.T, self_blocks, near_blocks, leaf_basis, transfer, parent_kernel, chain_coupling)
     return pl.pallas_call(
         hand_out,
         out_shape=tuple(jax.ShapeDtypeStruct(r.shape, r.dtype) for r in results),

time: 76.2 us -> 74.4 us (0.976); the launches traced: 74.9 us -> 74.2 us
  Pallas kernels: 72.1 us -> 73.6 us
  local copies, waits for them, and re-layouts: 1.41 us -> 0 us
    pallas_call x1, Pallas kernels: 70.5 us -> 72 us  [per_device(): pl.pallas_call(kernel_body, out_shape=(jax.ShapeDtypeStruct((leaves, RANK...]
    unnamed x3 -> x0, local copies, waits for them, and re-layouts: 1.41 us -> none
where the time goes in v4:
time: 74.4 us; the launch traced here: 74.2 us
  Pallas kernels  73.6 us (99%)
    pallas_call x1, Pallas kernels, per_device(): pl.pallas_call(kernel_body, out_shape=(jax.ShapeDtypeStruct((leaves, RANK...  72 us
    pallas_call x1, Pallas kernels, per_device(): pl.pallas_call(hand_out, out_shape=tuple((jax.ShapeDtypeStruct(r.shape, r...  1.65 us

profile of v4, /device:TPU:56, one launch (start us, length us, event | category | flops | bytes accessed | tf_op | source)
XLA Modules:
  0.0 74.2 jit_solution(18217373012046304898)
XLA Ops:
  0.6 72.0 %shard_map.103 = (f32[2,128,128]{2,1,0:T(8,128)}, f32[1,128,128]{2,1,0:T(8,128)}, f32[1,128,128]{2,1,0:T(8,128)}) custom-call(s32[2,16]{1,0:T(2,128)} %adm.1, s32[1,2]{1,0:T(1,128)} %bitcast.1, bf16[2,512,512]{2,1,0:T(8,128)(2,1)} %blocks_hbm.1, bf16[2,1,512,512]{3,2,1,0:T(8,128)(2,1)} %near_hbm.1, bf16[2,512,512]{2,1,0:T(8,128)(2,1)} %basis_hbm.1, ...), custom_call_target="tpu_custom_call" | custom-call | tf_op jit(solution)/shard_map/pallas_call | solution.py:532
  72.6 1.6 %shard_map.104 = (f32[2,128,128]{2,1,0:T(8,128)}, f32[1,128,128]{2,1,0:T(8,128)}, f32[1,128,128]{2,1,0:T(8,128)}) custom-call(f32[2,128,128]{2,1,0:T(8,128)} %get-tuple-element.6.refs_0_, f32[1,128,128]{2,1,0:T(8,128)} %get-tuple-element.7.refs_1_, f32[1,128,128]{2,1,0:T(8,128)} %get-tuple-element.8.refs_2_), custom_call_target="tpu_custom_call" | custom-call | tf_op jit(solution)/shard_map/pallas_call | solution.py:580

commit v5 on v4

--- a/solution.py
+++ b/solution.py
@@ -222,10 +222,10 @@
 
 
 def kernel_body(
-    adm, near_list, blocks_hbm, near_hbm, basis_hbm, transfer_hbm, kernel_hbm, chain_hbm,
+    adm_hbm, near_list_hbm, blocks_hbm, near_hbm, basis_hbm, transfer_hbm, kernel_hbm, chain_hbm,
     panels_hbm, parent_hbm, top_hbm,
     blocks, near, basis, transfer, upper, lower, halo, maps, reduced, inverses, lifted, terms, shares,
-    down_in, up_in, near_sum, far_in, facing, local_in, prefix, prefix_t, cross, slabs, slab_in, inverse, where, panels_ref, parent_ref, top_ref,
+    chain_in, near_sum, far_in, facing, local_in, prefix, prefix_t, cross, slabs, slab_in, inverse, where, panels_ref, parent_ref, top_ref, adm, near_list,
     load_sem, send_1, recv_1, send_2, recv_2, send_c, recv_c, send_f, recv_f, send_g, recv_g, send_r, recv_r, out_sem,
 ):
     at = Places()
@@ -245,15 +245,85 @@
     loads = [pltpu.make_async_copy(src, dst, load_sem.at[i]) for i, (src, dst) in enumerate(loads)]
     results = ((panels_ref, panels_hbm), (parent_ref, parent_hbm), (top_ref, top_hbm))
     results = [pltpu.make_async_copy(src, dst, out_sem.at[i]) for i, (src, dst) in enumerate(results)]
+    scalars = [
+        pltpu.make_async_copy(adm_hbm, adm, load_sem.at[2 * leaves + 6]),
+        pltpu.make_async_copy(near_list_hbm, near_list, load_sem.at[2 * leaves + 7]),
+    ]
     greet(at)
     loads[0].start()
     loads[1].start()
     await_greetings(at)
     exchange(at.z, at.on_z, lambda i: top, upper.at[at.y], send_1.at[0], recv_1.at[0])
     exchange(at.y, at.on_y, lambda i: bottom, lower.at[at.z], send_1.at[1], recv_1.at[1])
-    for load in loads[2 : 2 * leaves] + loads[-3:-1]:
+    for load in loads[2 : 2 * leaves] + loads[-3:-1] + scalars:
         load.start()
 
+    for l in range(leaves):
+        loads[2 * l].wait()
+        loads[2 * l + 1].wait()
+        form_reduced(l, parts, blocks, basis, reduced)
+
+    def gather_copies(t, u):
+        copies = []
+        piece = pl.ds(u * SPAN, SPAN)
+        for h, (table, pos, to) in enumerate(((upper, at.y, at.on_y), (lower, at.z, at.on_z))):
+            for up in range(2):
+                if t == SIZE and up == u % 2:
+                    continue
+                chunk = (pos - t + 1 + RING) % RING if up else (pos + t - 1) % RING
+                target = (pos + 1) % RING if up else (pos + RING - 1) % RING
+                part = table.at[chunk, piece]
+                copies.append(remote(part, part, send_2.at[h, up, t, u], recv_2.at[h, up, t, u], to(target)))
+        return copies
+
+    def halo_copies():
+        source = basis.at[:, :, skeleton]
+        return [
+            remote(source, halo.at[pl.ds(0, leaves)], send_1.at[0, 0], recv_1.at[0, 0], at.on_leaf(1)),
+            remote(source, halo.at[pl.ds(leaves, leaves)], send_1.at[1, 0], recv_1.at[1, 0], at.on_leaf(-1)),
+        ]
+
+    def first_copies():
+        return [
+            remote(top, upper.at[at.y, at.z], send_1.at[0, o], recv_1.at[0, o], at.on_z((at.z + o) % RING))
+            for o in range(1, RING)
+        ] + [
+            remote(bottom, lower.at[at.z, at.y], send_1.at[1, o], recv_1.at[1, o], at.on_y((at.y + o) % RING))
+            for o in range(1, RING)
+        ]
+
+    def between(k, s):
+        for (block, step), t, u in GATHER_AT:
+            if s == step:
+
+                @pl.when(k == block)
+                def _(t=t, u=u):
+                    for copy in gather_copies(t - 1, u):
+                        copy.wait_recv()
+                    for copy in gather_copies(t, u):
+                        copy.start()
+                    if (t, u) == (2, PIECES - 1):
+                        exchange(at.grp, at.on_grp, lambda i: chain_hbm.at[0], maps, send_1.at[2], recv_1.at[2])
+
+        if s == 4:
+
+            @pl.when(k == 1)
+            def _():
+                loads[2 * leaves].wait()
+                for l in range(leaves):
+                    facing[l] = dot_t(basis[l, :, skeleton], near[l, 0]).astype(bf16)
+
+    loads[-3].wait()
+    loads[-2].wait()
+    wait_all(first_copies())
+    for u in range(PIECES):
+        for copy in gather_copies(1, u):
+            copy.start()
+    for load in (loads[2 * leaves], loads[2 * leaves + 1], loads[-1]):
+        load.start()
+    eliminate(leaves, parts, reduced, inverses, between)
+
+    wait_all(scalars)
     column = lax.broadcasted_iota(jnp.int32, TILE, 1)
     row = lax.broadcasted_iota(jnp.int32, TILE, 0)
     places = jnp.full(TILE, leaves * entries, jnp.int32)
@@ -263,71 +333,6 @@
     inverse[...] = places
     to_scalars = pltpu.make_async_copy(inverse, where, load_sem.at[2 * leaves + 5])
     to_scalars.start()
-
-    for l in range(leaves):
-        loads[2 * l].wait()
-        loads[2 * l + 1].wait()
-        form_reduced(l, parts, blocks, basis, reduced)
-
-    def gather_copies(t, u):
-        copies = []
-        piece = pl.ds(u * SPAN, SPAN)
-        for h, (table, pos, to) in enumerate(((upper, at.y, at.on_y), (lower, at.z, at.on_z))):
-            for up in range(2):
-                if t == SIZE and not up:
-                    continue
-                chunk = (pos - t + 1 + RING) % RING if up else (pos + t - 1) % RING
-                target = (pos + 1) % RING if up else (pos + RING - 1) % RING
-                part = table.at[chunk, piece]
-                copies.append(remote(part, part, send_2.at[h, up, t, u], recv_2.at[h, up, t, u], to(target)))
-        return copies
-
-    def halo_copies():
-        source = basis.at[:, :, skeleton]
-        return [
-            remote(source, halo.at[pl.ds(0, leaves)], send_1.at[0, 0], recv_1.at[0, 0], at.on_leaf(1)),
-            remote(source, halo.at[pl.ds(leaves, leaves)], send_1.at[1, 0], recv_1.at[1, 0], at.on_leaf(-1)),
-        ]
-
-    def first_copies():
-        return [
-            remote(top, upper.at[at.y, at.z], send_1.at[0, o], recv_1.at[0, o], at.on_z((at.z + o) % RING))
-            for o in range(1, RING)
-        ] + [
-            remote(bottom, lower.at[at.z, at.y], send_1.at[1, o], recv_1.at[1, o], at.on_y((at.y + o) % RING))
-            for o in range(1, RING)
-        ]
-
-    def between(k, s):
-        for (block, step), t, u in GATHER_AT:
-            if s == step:
-
-                @pl.when(k == block)
-                def _(t=t, u=u):
-                    for copy in gather_copies(t - 1, u):
-                        copy.wait_recv()
-                    for copy in gather_copies(t, u):
-                        copy.start()
-                    if (t, u) == (2, PIECES - 1):
-                        exchange(at.grp, at.on_grp, lambda i: chain_hbm.at[0], maps, send_1.at[2], recv_1.at[2])
-
-        if s == 4:
-
-            @pl.when(k == 1)
-            def _():
-                loads[2 * leaves].wait()
-                for l in range(leaves):
-                    facing[l] = dot_t(basis[l, :, skeleton], near[l, 0]).astype(bf16)
-
-    loads[-3].wait()
-    loads[-2].wait()
-    wait_all(first_copies())
-    for u in range(PIECES):
-        for copy in gather_copies(1, u):
-            copy.start()
-    for load in (loads[2 * leaves], loads[2 * leaves + 1], loads[-1]):
-        load.start()
-    eliminate(leaves, parts, reduced, inverses, between)
 
     loads[2 * leaves + 1].wait()
     for l in range(leaves):
@@ -405,30 +410,31 @@
             shares[0, pz, py] = share[:HALF]
             shares[1, py, pz] = share[HALF:]
 
+    def chain_chunk(h, up, t):
+        pos, _ = lines[h]
+        return (pos + 5 - t) % RING if up else (pos - 5 + t + RING) % RING
+
+    def starts(up, t, u):
+        return t > 1 or up == u % 2
+
     def chain_copy(h, up, t, u):
         pos, to = lines[h]
         piece = pl.ds(u * SPAN, SPAN)
-        buffer = (down_in, up_in)[up]
-        chunk = (pos + 4 - t + RING) % RING if up else (pos - 5 + t + RING) % RING
-        src = shares.at[h, chunk, piece] if t == 1 else buffer.at[h, t - 2, piece]
+        src = chain_in.at[h, up, t - 2, piece] if starts(up, t - 1, u) and t > 1 else shares.at[h, chain_chunk(h, up, t), piece]
         target = (pos + 1) % RING if up else (pos + RING - 1) % RING
-        return remote(src, buffer.at[h, t - 1, piece], send_c.at[h, up, t, u], recv_c.at[h, up, t, u], to(target))
+        return remote(src, chain_in.at[h, up, t - 1, piece], send_c.at[h, up, t, u], recv_c.at[h, up, t, u], to(target))
 
     def chain_step(t):
         for u in range(PIECES):
+            piece = pl.ds(u * SPAN, SPAN)
             for h in range(2):
-                pos, _ = lines[h]
                 for up in range(2):
-                    if t > 1:
+                    if not starts(up, t, u):
+                        continue
+                    if t > 1 and starts(up, t - 1, u):
                         chain_copy(h, up, t - 1, u).wait_recv()
-                    if up and t == SIZE:
-                        continue
-                    if t > 1:
-                        piece = pl.ds(u * SPAN, SPAN)
-                        buffer = (down_in, up_in)[up]
-                        chunk = (pos + 4 - t + RING) % RING if up else (pos - 5 + t + RING) % RING
-                        mine = shares[h, chunk, piece].astype(f32)
-                        buffer[h, t - 2, piece] = (buffer[h, t - 2, piece].astype(f32) + mine).astype(bf16)
+                        mine = shares[h, chain_chunk(h, up, t), piece].astype(f32)
+                        chain_in[h, up, t - 2, piece] = (chain_in[h, up, t - 2, piece].astype(f32) + mine).astype(bf16)
                     chain_copy(h, up, t, u).start()
 
     chain_step(1)
@@ -477,10 +483,11 @@
         piece = pl.ds(u * SPAN, SPAN)
         for h in range(2):
             pos, _ = lines[h]
-            chain_copy(h, 0, SIZE, u).wait_recv()
+            for up in range(2):
+                chain_copy(h, up, SIZE, u).wait_recv()
             near_sum[h, piece] = (
-                down_in[h, SIZE - 1, piece].astype(f32)
-                + up_in[h, SIZE - 2, piece].astype(f32)
+                chain_in[h, 0, SIZE - 1, piece].astype(f32)
+                + chain_in[h, 1, SIZE - 1, piece].astype(f32)
                 + shares[h, pos, piece].astype(f32)
             ).astype(bf16)
             for i in range(u * SPAN, (u + 1) * SPAN):
@@ -503,9 +510,10 @@
     results[2].start()
     for h in range(2):
         for up in range(2):
-            for t in range(1, SIZE + 1 - up):
+            for t in range(1, SIZE + 1):
                 for u in range(PIECES):
-                    chain_copy(h, up, t, u).wait_send()
+                    if starts(up, t, u):
+                        chain_copy(h, up, t, u).wait_send()
     for h in range(2):
         other, to = lines[1 - h]
         total = near_sum[h, other].astype(f32)
@@ -532,7 +540,7 @@
     results = pl.pallas_call(
         kernel_body,
         out_shape=(jax.ShapeDtypeStruct((leaves, RANK, RANK), f32), panel, panel),
-        in_specs=[SMEM] * 2 + [HBM] * 6,
+        in_specs=[HBM] * 8,
         out_specs=(HBM,) * 3,
         scratch_shapes=[
             pltpu.VMEM((leaves, width, width), bf16),
@@ -548,8 +556,7 @@
             pltpu.VMEM((leaves * entries, RANK, RANK), bf16),
             pltpu.VMEM((leaves * entries + 1, RANK, RANK), bf16),
             pltpu.VMEM((2, RING, RING, HALF, RANK), bf16),
-            pltpu.VMEM((2, SIZE, RING, HALF, RANK), bf16),
-            pltpu.VMEM((2, SIZE - 1, RING, HALF, RANK), bf16),
+            pltpu.VMEM((2, 2, SIZE, RING, HALF, RANK), bf16),
             pltpu.VMEM((2, RING, HALF, RANK), bf16),
             pltpu.VMEM((2, RING, HALF, RANK), bf16),
             pltpu.VMEM((leaves, RANK, width), bf16),
@@ -564,7 +571,9 @@
             pltpu.VMEM((leaves, RANK, RANK), f32),
             pltpu.VMEM((1, RANK, RANK), f32),
             pltpu.VMEM((1, RANK, RANK), f32),
-            sems((2 * leaves + 6,)),
+            pltpu.SMEM((leaves, entries), jnp.int32),
+            pltpu.SMEM((1, leaves), jnp.int32),
+            sems((2 * leaves + 8,)),
             sems((3, RING)), sems((3, RING)),
             sems((2, 2, SIZE + 1, PIECES)), sems((2, 2, SIZE + 1, PIECES)),
             sems((2, 2, SIZE + 1, PIECES)), sems((2, 2, SIZE + 1, PIECES)),

time: 74.4 us -> 73.8 us (level); the launches traced: 74.2 us -> 72.7 us
  Pallas kernels: 73.6 us -> 72.1 us
    pallas_call x1, Pallas kernels: 72 us -> 70.4 us  [per_device(): pl.pallas_call(kernel_body, out_shape=(jax.ShapeDtypeStruct((leaves, RANK...]
where the time goes in v5:
time: 73.8 us; the launch traced here: 72.7 us
  Pallas kernels  72.1 us (98%)
    pallas_call x1, Pallas kernels, per_device(): pl.pallas_call(kernel_body, out_shape=(jax.ShapeDtypeStruct((leaves, RANK...  70.4 us
    pallas_call x1, Pallas kernels, per_device(): pl.pallas_call(hand_out, out_shape=tuple((jax.ShapeDtypeStruct(r.shape, r...  1.65 us

profile of v5, /device:TPU:56, one launch (start us, length us, event | category | flops | bytes accessed | tf_op | source)
XLA Modules:
  0.0 72.7 jit_solution(1004521957231956720)
XLA Ops:
  0.6 70.4 %shard_map.103 = (f32[2,128,128]{2,1,0:T(8,128)}, f32[1,128,128]{2,1,0:T(8,128)}, f32[1,128,128]{2,1,0:T(8,128)}) custom-call(s32[2,16]{1,0:T(2,128)} %adm_hbm.1, s32[1,2]{1,0:T(1,128)} %bitcast.1, bf16[2,512,512]{2,1,0:T(8,128)(2,1)} %blocks_hbm.1, bf16[2,1,512,512]{3,2,1,0:T(8,128)(2,1)} %near_hbm.1, bf16[2,512,512]{2,1,0:T(8,128)(2,1)} %basis_hbm.1, ...), custom_call_target="tpu_custom_call" | custom-call | tf_op jit(solution)/shard_map/pallas_call | solution.py:540
  71.1 1.6 %shard_map.104 = (f32[2,128,128]{2,1,0:T(8,128)}, f32[1,128,128]{2,1,0:T(8,128)}, f32[1,128,128]{2,1,0:T(8,128)}) custom-call(f32[2,128,128]{2,1,0:T(8,128)} %get-tuple-element.6.refs_0_, f32[1,128,128]{2,1,0:T(8,128)} %get-tuple-element.7.refs_1_, f32[1,128,128]{2,1,0:T(8,128)} %get-tuple-element.8.refs_2_), custom_call_target="tpu_custom_call" | custom-call | tf_op jit(solution)/shard_map/pallas_call | solution.py:589
